TPU v7x, 256 devices: a whole 4x4x8 slice. The times are simulated.
256 devices in a mesh: row: 8 (over x, z_hi), col: 32 (over y, z_lo, core).
Axes of the slice: x: 4, y: 4, z: 8 (z_hi: 2, z_lo: 4; z = z_hi * 4 + z_lo), core: 2. Of those that a mesh axis runs over, the one named last changes fastest.
Arguments:
- activations: bfloat16 [512, 8192], P('col', 'row'), may hold values from -22 to 22
- out_grad: bfloat16 [512, 8192], P('col', 'row'), may hold values from -2 to 2
- norm_gain: float32 [8192], P('row'), may hold values from 0.5 to 1.5
- gate_weight: bfloat16 [8192, 28672], P('row', 'col'), may hold values from -0.0625 to 0.0625
- up_weight: bfloat16 [8192, 28672], P('row', 'col'), may hold values from -0.0625 to 0.0625
- down_weight: bfloat16 [28672, 8192], P('col', 'row'), may hold values from -0.03125 to 0.03125
Outputs:
- grad_input: bfloat16 [512, 8192], P('col', 'row')
- grad_gain: float32 [8192], P('row')
- grad_gate: bfloat16 [8192, 28672], P('row', 'col')
- grad_up: bfloat16 [8192, 28672], P('row', 'col')
- grad_down: bfloat16 [28672, 8192], P('col', 'row')
All inputs are finite; a program needn't handle non-finite values.
Results may differ from a plain program's by a relative error of at most 0.0067.
Values may be sent and summed in bfloat16 or wider, within the bound.
No kernel may reach another device: no remote copies, remote signals or barrier semaphores. Data moves between devices by JAX's collectives and lax.ppermute only.
A program may use at most 64 MiB of HBM per device.

v0:
```python
import jax
import jax.numpy as jnp
from jax import lax
from jax.sharding import PartitionSpec as P

D = 8192


def swiglu_grads(sums, width):
    gate = sums[:, :width]
    up = sums[:, width : 2 * width]
    back = sums[:, 2 * width :]
    sig = jax.nn.sigmoid(gate)
    silu = gate * sig
    d_gate = back * up * sig * (1.0 + gate * (1.0 - sig))
    d_up = back * silu
    hidden = silu * up
    return jnp.concatenate(
        [d_gate.astype(jnp.bfloat16), d_up.astype(jnp.bfloat16), hidden.astype(jnp.bfloat16)],
        axis=1,
    )


def shards(activations, out_grad, norm_gain, gate_weight, up_weight, down_weight):
    x_full = activations.astype(jnp.float32)
    sq_sum = lax.psum(jnp.sum(x_full * x_full, axis=1), "row")
    inv_rms = lax.rsqrt(sq_sum / D + 1e-05)[:, None]
    normed = (x_full * inv_rms * norm_gain).astype(jnp.bfloat16)
    normed_all, grad_all = (
        lax.all_gather(normed, "col", axis=0, tiled=True),
        lax.all_gather(out_grad, "col", axis=0, tiled=True),
    )
    width = gate_weight.shape[1]
    contract_last = (((1,), (1,)), ((), ()))
    summed = lax.psum(
        jnp.concatenate(
            [
                jnp.dot(normed_all, gate_weight, preferred_element_type=jnp.float32),
                jnp.dot(normed_all, up_weight, preferred_element_type=jnp.float32),
                lax.dot_general(
                    grad_all, down_weight, contract_last, preferred_element_type=jnp.float32
                ),
            ],
            axis=1,
        ),
        "row",
    )
    stacked = swiglu_grads(summed, width)
    d_gate = stacked[:, :width]
    d_up = stacked[:, width : 2 * width]
    hidden = stacked[:, 2 * width :]
    contract_first = (((0,), (0,)), ((), ()))
    grad_gate = lax.dot_general(
        normed_all, d_gate, contract_first, preferred_element_type=jnp.float32
    ).astype(jnp.bfloat16)
    grad_up = lax.dot_general(
        normed_all, d_up, contract_first, preferred_element_type=jnp.float32
    ).astype(jnp.bfloat16)
    grad_down = lax.dot_general(
        hidden, grad_all, contract_first, preferred_element_type=jnp.float32
    ).astype(jnp.bfloat16)
    grad_normed = lax.psum_scatter(
        lax.dot_general(d_gate, gate_weight, contract_last, preferred_element_type=jnp.float32)
        + lax.dot_general(d_up, up_weight, contract_last, preferred_element_type=jnp.float32),
        "col",
        scatter_dimension=0,
        tiled=True,
    )
    grad_gain = lax.psum(jnp.sum(grad_normed * x_full * inv_rms, axis=0), "col")
    scaled = grad_normed * norm_gain
    mean_term = lax.psum(jnp.sum(scaled * x_full, axis=1), "row")[:, None] / D
    grad_input = (inv_rms * scaled - x_full * inv_rms * inv_rms * inv_rms * mean_term).astype(
        jnp.bfloat16
    )
    return (grad_input, grad_gain, grad_gate, grad_up, grad_down)


def solution(mesh):
    in_specs = (
        P("col", "row"),
        P("col", "row"),
        P("row"),
        P("row", "col"),
        P("row", "col"),
        P("col", "row"),
    )
    out_specs = (P("col", "row"), P("row"), P("row", "col"), P("row", "col"), P("col", "row"))
    return jax.shard_map(shards, mesh=mesh, in_specs=in_specs, out_specs=out_specs, check_vma=False)
```

profile of v0, /device:TPU:4, one launch (start us, length us, event | category | flops | bytes accessed | tf_op | source)
XLA Modules:
  0.0 869.2 jit_solution(8081157554624035636)
XLA Ops:
  7.2 1.0 fusion.9
  8.2 28.9 %psum.28 = f32[16]{0:T(128)S(1)} all-reduce(f32[16]{0:T(128)S(1)} %fusion.9), channel_id=1, replica_groups=mesh['row'=8,'col'=32] {'row'}, use_global_device_ids=true, to_apply=%region_1.0 | all-reduce | flops 16 | bytes 128 | tf_op jit(solution)/shard_map/psum | solution.py:26
  37.1 1.5 fusion.4
  38.6 0.7 all-gather.5.cloned.1.call-update
  39.4 57.9 %all-gather.3.cloned.1.call-done = bf16[512,1024]{1,0:T(8,128)(2,1)} async-done(((bf16[16,1024]{1,0:T(8,128)(2,1)}), bf16[512,1024]{1,0:T(8,128)(2,1)}) %all-gather.3.cloned.1.call-update) | async-done | bytes 1048592 | tf_op jit(solution)/shard_map/all_gather | solution.py:30
  97.2 4.4 fusion.15
  101.6 2.5 fusion.14
  104.1 52.8 %all-gather.5.cloned.1.call-done = bf16[512,1024]{1,0:T(8,128)(2,1)} async-done(((bf16[16,1024]{1,0:T(8,128)(2,1)}), bf16[512,1024]{1,0:T(8,128)(2,1)}) %all-gather.5.cloned.1.call-update) | async-done | bytes 1048592 | tf_op jit(solution)/shard_map/all_gather | solution.py:31
  156.9 3.2 fusion.16
  160.2 2.8 pad_maximum_fusion
  163.0 0.0 reduce-scatter.2.cloned.1.call-start
  163.1 449.2 %all-reduce.2.cloned.1.call-done = f32[512,2688]{1,0:T(8,128)} async-done(((f32[512,2688]{1,0:T(8,128)}), f32[512,2688]{1,0:T(8,128)}) %all-reduce.2.cloned.1.call-update) | async-done | bytes 5505040 | tf_op jit(solution)/shard_map/psum | solution.py:35
  612.3 3.5 multiply_convert_fusion.1
  615.8 1.3 fusion.17
  617.1 0.5 copy-done.6
  617.6 2.7 convolution_add_fusion
  620.3 4.1 convolution_convert_fusion.1
  624.4 2.5 convolution_convert_fusion.2
  626.9 4.6 convolution_convert_fusion
  631.5 133.2 %reduce-scatter.2.cloned.1.call-done = f32[16,1024]{1,0:T(8,128)} async-done(((f32[512,1024]{1,0:T(8,128)}), f32[16,1024]{1,0:T(8,128)}) %reduce-scatter.2.cloned.1.call-update) | async-done | bytes 65552 | tf_op jit(solution)/shard_map/reduce_scatter | solution.py:62
  764.7 1.0 fusion.12
  765.7 68.2 %psum.31 = f32[1024]{0:T(1024)} all-reduce(f32[1024]{0:T(1024)S(1)} %get-tuple-element.5), channel_id=1, replica_groups=mesh['row'=8,'col'=32] {'col'}, use_global_device_ids=true, to_apply=%region_7.0 | all-reduce | flops 1024 | bytes 8192 | tf_op jit(solution)/shard_map/psum | solution.py:69
  833.9 27.2 %psum.30 = f32[16]{0:T(128)S(1)} all-reduce(f32[16]{0:T(128)S(1)} %get-tuple-element.6), channel_id=1, replica_groups=mesh['row'=8,'col'=32] {'row'}, use_global_device_ids=true, to_apply=%region_5.0 | all-reduce | flops 16 | bytes 128 | tf_op jit(solution)/shard_map/psum | solution.py:71
  861.1 1.5 fusion.8
  (27 shorter events, 0.2 us)
Async XLA Ops:
  7.2 94.5 %copy-start = (bf16[1024,896]{1,0:T(8,128)(2,1)S(1)}, bf16[1024,896]{1,0:T(8,128)(2,1)}, u32[]{:S(2)}) copy-start(bf16[1024,896]{1,0:T(8,128)(2,1)} %param.9) | copy-start | bytes 5505028
  7.2 90.1 %all-gather.3.cloned.1.call-start = ((), (), s32[]{:S(2)}) async-start(), calls=%async_computation.1 | async-start | bytes 1081344 | tf_op jit(solution)/shard_map/all_gather | solution.py:30
  38.6 118.3 %all-gather.5.cloned.1.call-start = ((), (), s32[]{:S(2)}) async-start(), calls=%async_computation.2 | async-start | bytes 1081344 | tf_op jit(solution)/shard_map/all_gather | solution.py:31
  39.3 572.9 %all-reduce.2.cloned.1.call-start = ((), (), s32[]{:S(2)}) async-start(), calls=%async_computation.3 | async-start | bytes 11010048 | tf_op jit(solution)/shard_map/psum | solution.py:35
  97.2 4.4 copy-start.7
  156.9 3.3 copy-start.1
  156.9 3.3 copy-start.2
  163.0 601.7 %reduce-scatter.2.cloned.1.call-start = ((), (), s32[]{:S(2)}) async-start(), calls=%async_computation.4 | async-start | bytes 2162688 | tf_op jit(solution)/shard_map/reduce_scatter | solution.py:62
  615.8 1.3 copy-start.3
  615.8 1.8 copy-start.6
  620.3 4.1 copy-start.8
  624.4 2.5 copy-start.9
  626.9 137.7 %copy-start.4 = (bf16[16,1024]{1,0:T(8,128)(2,1)S(1)}, bf16[16,1024]{1,0:T(8,128)(2,1)}, u32[]{:S(2)}) copy-start(bf16[16,1024]{1,0:T(8,128)(2,1)} %param.6) | copy-start | bytes 98308
  626.9 137.8 %copy-start.5 = (f32[1024]{0:T(1024)S(1)}, f32[1024]{0:T(1024)}, u32[]{:S(2)}) copy-start(f32[1024]{0:T(1024)} %param.8) | copy-start | bytes 12292
Sparse Core Ops, SparseCore 0:
  38.7 58.4 all-gather.2
  99.1 57.7 all-gather.4
  163.1 449.1 all-reduce.1
  620.4 144.2 reduce-scatter.1
where the time goes:
time: 872 us; the launch traced here: 869 us
  waiting for transfers between devices  694 us (80%)
  blocking collectives  124 us (14%)
  matrix products  25.3 us (3%)
  between operations  13.8 us (2%)
  other arithmetic  11.3 us (1%)
    psum x1, waiting for transfers between devices, shards(): lax.psum(jnp.concatenate([jnp.dot(normed_all, gate_weight, preferred_elem...  449 us
    reduce_scatter x1, waiting for transfers between devices, shards(): lax.psum_scatter(lax.dot_general(d_gate, gate_weight, contract_last, pref...  133 us
    psum x1, blocking collectives, shards(): grad_gain = lax.psum(jnp.sum(grad_normed * x_full * inv_rms, axis=0), 'col')  68.2 us
    all_gather x1, waiting for transfers between devices, shards(): lax.all_gather(normed, 'col', axis=0, tiled=True)  57.9 us
    all_gather x1, waiting for transfers between devices, shards(): lax.all_gather(out_grad, 'col', axis=0, tiled=True)  52.8 us
    psum x1, blocking collectives, shards(): sq_sum = lax.psum(jnp.sum(x_full * x_full, axis=1), 'row')  28.9 us
    psum x1, blocking collectives, shards(): mean_term = lax.psum(jnp.sum(scaled * x_full, axis=1), 'row')[:, None] / D  27.2 us
  transfers between devices with their start and end apart: 4, of which 4 were waited for; matrix products, arithmetic and copies ran while one was open for 2% of the time, Pallas kernels for 0%

commit v1 on v0

v1 whole, which is shorter than its diff:
```python
import jax
import jax.numpy as jnp
from jax import lax
from jax.experimental import pallas as pl
from jax.experimental.pallas import tpu as pltpu
from jax.sharding import Mesh
from jax.sharding import PartitionSpec as P

D = 8192
BF = jnp.bfloat16
F32 = jnp.float32
LANES = 128
AXES = ("x", "zh", "y", "zl", "core")
CONTRACT_LAST = (((1,), (1,)), ((), ()))
CONTRACT_FIRST = (((0,), (0,)), ((), ()))
STEPS = (0, 1, -1, 2)
PARTS = 4
EXTRA = 16
GROUPS = ((0, 1), (2, 3))
GAINS = GROUPS[-1]


def ring(size, step):
    return [(i, (i + step) % size) for i in range(size)]


def send(value, axis, step):
    return lax.ppermute(value, axis, ring(2 if axis in ("zh", "core") else 4, step))


def tail(*columns):
    lane = lax.broadcasted_iota(jnp.int32, (columns[0].shape[0], LANES), 1)
    out = jnp.zeros((columns[0].shape[0], LANES), F32)
    at = 0
    for rest in columns:
        for _ in range(3):
            piece = rest.astype(BF).astype(F32)
            out = jnp.where(lane == at, piece, out)
            rest = rest - piece
            at += 1
    return out


def head(block, at):
    return block[:, at : at + 1] + block[:, at + 1 : at + 2] + block[:, at + 2 : at + 3]


def call(kernel, out_shapes, args, limit=24, flops=0):
    return pl.pallas_call(
        kernel,
        out_shape=[jax.ShapeDtypeStruct(s, d) for s, d in out_shapes],
        compiler_params=pltpu.CompilerParams(vmem_limit_bytes=limit * 1024 * 1024),
    )(*args)


def load(weights):
    count = len(weights)

    def kernel(*refs):
        sems, copies = refs[-1], []
        for n, (source, target) in enumerate(zip(refs[:count], refs[count : 2 * count])):
            step = source.shape[0] // PARTS
            for p in range(PARTS):
                rows = pl.ds(p * step, step)
                copies.append(
                    pltpu.make_async_copy(source.at[rows], target.at[rows], sems.at[n, p])
                )
        for copy in copies:
            copy.start()
        for copy in copies:
            copy.wait()

    return pl.pallas_call(
        kernel,
        out_shape=[jax.ShapeDtypeStruct(w.shape, w.dtype) for w in weights],
        in_specs=[pl.BlockSpec(memory_space=pltpu.HBM)] * count,
        out_specs=[pl.BlockSpec(memory_space=pltpu.VMEM)] * count,
        scratch_shapes=[pltpu.SemaphoreType.DMA((count, PARTS))],
        compiler_params=pltpu.CompilerParams(vmem_limit_bytes=24 * 1024 * 1024),
    )(*[pltpu.with_memory_space_constraint(w, pltpu.HBM) for w in weights])


def split(row):
    line = lax.broadcasted_iota(jnp.int32, (EXTRA, row.shape[1]), 0)
    out = jnp.zeros((EXTRA, row.shape[1]), F32)
    for at in range(3):
        piece = row.astype(BF).astype(F32)
        out = jnp.where(line == at, piece, out)
        row = row - piece
    return out.astype(BF)


def joined(block):
    block = block.astype(F32)
    return block[0:1] + block[1:2] + block[2:3]


def label(slot):
    return lax.rem(lax.axis_index("x") + slot, 4)


def tokens(blocks, which):
    at = [label(s) for s in range(4)]
    return jnp.concatenate(
        [ref[at[s], which] for s in range(4) for pair in blocks for ref in pair], axis=0
    )


def pairs(refs):
    return [(refs[i], refs[i + 1]) for i in range(0, len(refs), 2)]


def forward(size, *refs):
    blocks, (gain, gate_w, up_w, down_w, *outs) = pairs(refs[: 2 * size]), refs[2 * size :]
    x = tokens(blocks, 0).astype(F32)
    scaled = (x * gain[...]).astype(BF)
    grad = tokens(blocks, 1)
    rows, width = 32 * size, gate_w.shape[1]

    def put(value, start):
        for s in range(4):
            part = value[rows * s : rows * s + rows]
            outs[s][:, start : start + value.shape[1]] = part.astype(outs[s].dtype)

    put(jnp.dot(scaled, gate_w[...], preferred_element_type=F32), 0)
    put(jnp.dot(scaled, up_w[...], preferred_element_type=F32), width)
    put(
        lax.dot_general(grad, down_w[...], CONTRACT_LAST, preferred_element_type=F32),
        2 * width,
    )
    put(tail(jnp.sum(x * x, axis=1, keepdims=True)), 3 * width)


def add_x(own, a, b, c, total, out):
    value = own[...] + a[...].astype(F32) + b[...].astype(F32) + c[...].astype(F32)
    end = tail(head(value[:, -LANES:], 0))
    value = jnp.concatenate([value[:, :-LANES], end], axis=1)
    total[...] = value
    out[...] = value.astype(BF)


def activate(own, other, out):
    total = own[...] + other[...].astype(F32)
    width = (total.shape[1] - LANES) // 3
    inv = lax.rsqrt(head(total[:, -LANES:], 0) / D + 1e-05)
    gate = total[:, :width] * inv
    up = total[:, width : 2 * width] * inv
    back = total[:, 2 * width : 3 * width]
    sig = 1.0 / (1.0 + jnp.exp(-gate))
    silu = gate * sig
    d_gate = back * up * sig * (1.0 + gate * (1.0 - sig))
    d_up = back * silu
    mean = jnp.sum(d_gate * gate + d_up * up, axis=1, keepdims=True)
    out[:, :width] = d_gate.astype(BF)
    out[:, width : 2 * width] = d_up.astype(BF)
    out[:, 2 * width : 3 * width] = (silu * up).astype(BF)
    out[:, 3 * width :] = tail(inv, mean).astype(BF)


def backward(size, *refs):
    messages, blocks = refs[:4], pairs(refs[4 : 4 + 2 * size])
    gate_w, up_w, last_gain, mine, theirs, inv_out, gain_out = refs[4 + 2 * size :]
    rows, (depth, width) = 32 * size, gate_w.shape

    def rows_of(start, stop):
        return jnp.concatenate([m[:, start:stop] for m in messages], axis=0)

    part = lax.dot_general(
        rows_of(0, width), gate_w[...], CONTRACT_LAST, preferred_element_type=F32
    ) + lax.dot_general(
        rows_of(width, 2 * width), up_w[...], CONTRACT_LAST, preferred_element_type=F32
    )
    end = rows_of(3 * width, 3 * width + LANES).astype(F32)
    inv = head(end, 0)
    mean = tail(head(end, 3))
    x = tokens(blocks, 0).astype(F32)
    gain = last_gain[...] + jnp.sum(part * x * inv, axis=0, keepdims=True)
    for s in range(4):
        at = label(s)
        inv_out[at] = inv[rows * s : rows * s + rows]
        for i in range(size):
            place = pl.ds(pl.multiple_of(64 * i + 16 * at, 16), 16)
            for core, out in enumerate((mine, theirs)):
                start = rows * s + 32 * i + 16 * core
                out[place, :depth] = part[start : start + 16]
                out[place, depth:] = mean[start : start + 16]
    gain_out[...] = gain
    theirs[64 * size :, :depth] = jnp.broadcast_to(gain, (8, depth))
    theirs[64 * size :, depth:] = jnp.zeros((8, LANES), F32)


def add_core(*refs):
    count = len(GROUPS)
    mine, received, gains, outs = refs[:count], refs[count : 2 * count], refs[-5], refs[-4:]
    depth = gains.shape[1]
    last = 64 * len(GROUPS[-1])
    gain = gains[...] + received[-1][last : last + 1, :depth]
    for g, group in enumerate(GROUPS):
        for i, block in enumerate(group):
            rows = slice(64 * i, 64 * i + 64)
            value, out = mine[g][rows] + received[g][rows], outs[block]
            out[:64, :depth] = value[:, :depth].astype(BF)
            out[:64, depth:] = tail(head(value[:, depth:], 0)).astype(BF)
            out[64:, :depth] = split(gain)
            out[64:, depth:] = jnp.zeros((EXTRA, LANES), BF)


def add_y(*refs):
    parts, outs = refs[:4], refs[4:]
    depth = parts[0].shape[1] - LANES
    total = sum(p[:64].astype(F32) for p in parts)
    gain = sum(joined(p[64:, :depth]) for p in parts)
    outs[0][:16] = total[:16]
    outs[0][16:, :depth] = jnp.broadcast_to(gain, (EXTRA, depth))
    outs[0][16:, depth:] = jnp.zeros((EXTRA, LANES), F32)
    for s in range(1, 4):
        outs[s][:16, :depth] = total[16 * s : 16 * s + 16, :depth].astype(BF)
        outs[s][:16, depth:] = tail(head(total[16 * s : 16 * s + 16, depth:], 0)).astype(BF)
        outs[s][16:, :depth] = split(gain)
        outs[s][16:, depth:] = jnp.zeros((EXTRA, LANES), BF)


def finish(own, a, b, c, x, inv, gain, grad_input, grad_gain):
    depth = x.shape[1]
    total = own[:16] + sum(v[:16].astype(F32) for v in (a, b, c))
    inv = inv[0, :16]
    mean = head(total[:, depth:], 0) / D
    grad_gain[...] = own[16:17, :depth] + sum(joined(v[16:, :depth]) for v in (a, b, c))
    grad_input[...] = (
        inv * total[:, :depth] * gain[...] - x[...].astype(F32) * inv * inv * mean
    ).astype(BF)


def wide_grads(at, *refs):
    count = len(GROUPS)
    messages, blocks = refs[: 4 * count], pairs(refs[4 * count : 4 * count + 8])
    invs, (gain, out) = refs[4 * count + 8 : -2], refs[-2:]
    width = out.shape[1]
    normed = []
    for g, group in enumerate(GROUPS):
        members = [blocks[i] for i in group]
        inv = jnp.concatenate([invs[g][label(s)] for s in range(4)], axis=0)
        normed.append((tokens(members, 0).astype(F32) * inv * gain[...]).astype(BF))
    columns = jnp.concatenate([m[:, at * width : at * width + width] for m in messages], axis=0)
    out[...] = lax.dot_general(
        jnp.concatenate(normed, axis=0), columns, CONTRACT_FIRST, preferred_element_type=F32
    ).astype(BF)


def down_grads(*refs):
    count = len(GROUPS)
    messages, blocks, out = refs[: 4 * count], pairs(refs[4 * count : -1]), refs[-1]
    width = out.shape[0]
    grads = jnp.concatenate([tokens([blocks[i] for i in g], 1) for g in GROUPS], axis=0)
    hidden = jnp.concatenate([m[:, 2 * width : 3 * width] for m in messages], axis=0)
    out[...] = lax.dot_general(
        hidden, grads, CONTRACT_FIRST, preferred_element_type=F32
    ).astype(BF)


def after(value, *earlier):
    return lax.optimization_barrier((value, *earlier))[0]


def shards(activations, out_grad, norm_gain, gate_w, up_w, down_w):
    rows, depth = activations.shape
    width = gate_w.shape[1]
    wide, deep = 3 * width + LANES, depth + LANES
    gain = norm_gain[None, :]

    gate_w, up_w, down_w = load([gate_w, up_w, down_w])
    both = jnp.stack([activations, out_grad])
    home = jnp.stack([both] + [send(both, "zl", -k) for k in (1, 2, 3)])
    own = [home] + [send(home, "y", s) for s in STEPS[1:]]
    own[1] = after(own[1], gate_w, up_w, down_w)
    other = [send(o, "core", 1) for o in own]

    def members(group):
        return [v for i in group for v in (own[i], other[i])]

    unit = 2 * depth * width * 128
    totals, crossed = [], []
    for group in GROUPS:
        tall = 32 * len(group)
        s0, s1, s2, s3 = call(
            lambda *a, n=len(group): forward(n, *a),
            [((tall, wide), F32)] + [((tall, wide), BF)] * 3,
            [*members(group), gain, gate_w, up_w, down_w],
            flops=3 * unit * len(group),
        )
        total, out = call(
            add_x,
            [((tall, wide), F32), ((tall, wide), BF)],
            [s0, send(s1, "x", 1), send(s2, "x", 2), send(s3, "x", -1)],
        )
        totals.append(total)
        crossed.append(send(out, "zh", 1))

    messages, invs, halves = [], [], []
    gains = jnp.zeros((1, depth), F32)
    for group, total, arrived in zip(GROUPS, totals, crossed):
        size = len(group)
        tall = 32 * size
        (m0,) = call(activate, [((tall, wide), BF)], [total, arrived])
        found = [m0, send(m0, "x", -1), send(m0, "x", 2), send(m0, "x", 1)]
        mine, theirs, inv, gains = call(
            lambda *a, n=size: backward(n, *a),
            [((64 * size, deep), F32), ((64 * size + 8, deep), F32), ((4, tall, 1), F32)]
            + [((1, depth), F32)],
            [*found, *members(group), gate_w, up_w, gains],
            flops=2 * unit * size,
        )
        halves.append((mine, send(theirs, "core", 1)))
        messages += found
        invs.append(inv)

    parts = call(
        add_core,
        [((64 + EXTRA, deep), BF)] * 4,
        [*[h[0] for h in halves], *[h[1] for h in halves], gains],
    )
    parts = [parts[0]] + [send(parts[i], "y", -STEPS[i]) for i in (1, 2, 3)]
    outs = call(
        add_y, [((16 + EXTRA, deep), F32)] + [((16 + EXTRA, deep), BF)] * 3, parts
    )
    flat = [v for pair in zip(own, other) for v in pair]
    (grad_down,) = call(
        down_grads, [((width, depth), BF)], [*messages, *flat], limit=32, flops=4 * unit
    )
    grad_gate, grad_up = (
        call(
            lambda *a, n=at: wide_grads(n, *a),
            [((depth, width), BF)],
            [*messages, *flat, *invs, gain],
            limit=32,
            flops=4 * unit,
        )[0]
        for at in (0, 1)
    )
    home_sums = [outs[0]]
    home_sums += [send(after(outs[k], grad_down, grad_up), "zl", k) for k in (1, 2, 3)]
    grad_input, grad_gain = call(
        finish,
        [((rows, depth), BF), ((1, depth), F32)],
        [*home_sums, activations, invs[0], gain],
    )
    return (grad_input, grad_gain[0], grad_gate, grad_up, grad_down)


def solution(mesh):
    fine = Mesh(mesh.devices.reshape(4, 2, 4, 4, 2), AXES)
    row, col = ("x", "zh"), ("y", "zl", "core")
    in_specs = (P(col, row), P(col, row), P(row), P(row, col), P(row, col), P(col, row))
    out_specs = (P(col, row), P(row), P(row, col), P(row, col), P(col, row))
    return jax.shard_map(shards, mesh=fine, in_specs=in_specs, out_specs=out_specs, check_vma=False)
```

time: 872 us -> 135 us (0.15)
  waiting for transfers between devices: 694 us -> 59.2 us
  blocking collectives: 124 us -> 0 us
  starting transfers between devices: 0.16 us -> 52.4 us
  matrix products: 25.3 us -> 0 us
  Pallas kernels: 0 us -> 19.5 us
  between operations: 13.8 us -> 0.8 us
  other arithmetic: 11.3 us -> 0.82 us
    psum x1 -> x0, waiting for transfers between devices: 449 us -> none  [shards(): lax.psum(jnp.concatenate([jnp.dot(normed_all, gate_weight, preferred_elem...]
    reduce_scatter x1 -> x0, waiting for transfers between devices: 133 us -> none  [shards(): lax.psum_scatter(lax.dot_general(d_gate, gate_weight, contract_last, pref...]
    psum x3 -> x0, blocking collectives: 124 us -> none  [the longest x1 68.2 us: shards(): grad_gain = lax.psum(jnp.sum(grad_normed * x_full * inv_rms, axis=0), 'col')]
    all_gather x2 -> x0, waiting for transfers between devices: 111 us -> none  [the longest x1 57.9 us: shards(): lax.all_gather(normed, 'col', axis=0, tiled=True)]
    ppermute x0 -> x32, waiting for transfers between devices: none -> 59.2 us  [send(): lax.ppermute(value, axis, ring(2 if axis in ('zh', 'core') else 4, step))]
    ppermute x0 -> x32, starting transfers between devices: none -> 52.4 us  [send(): lax.ppermute(value, axis, ring(2 if axis in ('zh', 'core') else 4, step))]
    dot_general x8 -> x0, matrix products: 25.3 us -> none  [the longest x1 4.55 us: shards(): lax.dot_general(hidden, grad_all, contract_first, preferred_element_type=...]
    pallas_call x0 -> x15, Pallas kernels: none -> 19.5 us  [the longest x14 16.8 us: call(): pl.pallas_call(kernel, out_shape=[jax.ShapeDtypeStruct(s, d) for s, d in...]
  transfers between devices with their start and end apart: 4 -> 32, of which waited for: 4 -> 19; matrix products, arithmetic and copies ran while one was open for 2% -> 0% of each run, Pallas kernels for 0% -> 13%
where the time goes in v1:
time: 135 us; the launch traced here: 133 us
  waiting for transfers between devices  59.2 us (44%)
  starting transfers between devices  52.4 us (39%)
  Pallas kernels  19.5 us (14%)
    ppermute x32, waiting for transfers between devices, send(): lax.ppermute(value, axis, ring(2 if axis in ('zh', 'core') else 4, step))  59.2 us
    ppermute x32, starting transfers between devices, send(): lax.ppermute(value, axis, ring(2 if axis in ('zh', 'core') else 4, step))  52.4 us
    pallas_call x14, Pallas kernels, call(): pl.pallas_call(kernel, out_shape=[jax.ShapeDtypeStruct(s, d) for s, d in...  16.8 us
  transfers between devices with their start and end apart: 32, of which 19 were waited for; matrix products, arithmetic and copies ran while one was open for 0% of the time, Pallas kernels for 13%

profile of v1, /device:TPU:4, one launch (start us, length us, event | category | flops | bytes accessed | tf_op | source)
XLA Modules:
  0.0 132.7 jit_solution(5060594893765283177)
XLA Ops:
  1.4 3.4 %collective-permute-start.1 = (bf16[2,16,1024]{2,1,0:T(8,128)(2,1)S(1)}, bf16[2,16,1024]{2,1,0:T(8,128)(2,1)S(1)}, u32[]{:S(2)}, u32[]{:S(2)}) collective-permute-start(bf16[2,16,1024]{2,1,0:T(8,128)(2,1)S(1)} %get-tuple-element.80), channel_id=1, source_target_pairs={{0,4},{2,6},{4,0},{6,2},{1,5},{3,7},{5,1},{7,3},{8,12},{10,14},{12... | collective-permute-start | bytes 196616 | tf_op jit(solution)/shard_map/ppermute | solution.py:28
  9.0 3.2 %collective-permute-done.2 = bf16[2,16,1024]{2,1,0:T(8,128)(2,1)S(1)} collective-permute-done((bf16[2,16,1024]{2,1,0:T(8,128)(2,1)S(1)}, bf16[2,16,1024]{2,1,0:T(8,128)(2,1)S(1)}, u32[]{:S(2)}, u32[]{:S(2)}) %collective-permute-start.2) | collective-permute-done | bytes 65568 | tf_op jit(solution)/shard_map/ppermute | solution.py:28
  14.0 2.6 %shard_map.101 = (bf16[1024,896]{1,0:T(8,128)(2,1)S(1)}, bf16[1024,896]{1,0:T(8,128)(2,1)S(1)}, bf16[896,1024]{1,0:T(8,128)(2,1)S(1)}) custom-call(bf16[1024,896]{1,0:T(8,128)(2,1)} %refs_0_.1, bf16[1024,896]{1,0:T(8,128)(2,1)} %refs_1_.1, bf16[896,1024]{1,0:T(8,128)(2,1)} %refs_2_.1), custom_call_target="tpu_custom_call" | custom-call | tf_op jit(solution)/shard_map/pallas_call | solution.py:73
  16.7 3.7 %collective-permute-done.4.a_2_.a_6_.refs_10_.a_10_ = bf16[4,2,16,1024]{3,2,1,0:T(8,128)(2,1)S(1)} collective-permute-done((bf16[4,2,16,1024]{3,2,1,0:T(8,128)(2,1)S(1)}, bf16[4,2,16,1024]{3,2,1,0:T(8,128)(2,1)S(1)}, u32[]{:S(2)}, u32[]{:S(2)}) %collective-permute-start.4) | collective-permute-done | bytes 262176 | tf_op jit(solution)/shard_map/ppermute | solution.py:28
  20.4 1.9 %collective-permute-start.15 = (bf16[4,2,16,1024]{3,2,1,0:T(8,128)(2,1)S(1)}, bf16[4,2,16,1024]{3,2,1,0:T(8,128)(2,1)S(1)}, u32[]{:S(2)}, u32[]{:S(2)}) collective-permute-start(bf16[4,2,16,1024]{3,2,1,0:T(8,128)(2,1)S(1)} %pad_maximum_fusion.a_0_.a_4_.refs_8_.a_8_), channel_id=1, source_target_pairs={{0,16},{8,24},{16,0},{24,8},{1,17},{9,25},{17,1},{25,9},{2,18},{10... | collective-permute-start | bytes 786440 | tf_op jit(solution)/shard_map/ppermute | solution.py:28
  23.4 1.8 %shard_map.102 = (f32[64,2816]{1,0:T(8,128)S(1)}, bf16[64,2816]{1,0:T(8,128)(2,1)S(1)}, bf16[64,2816]{1,0:T(8,128)(2,1)S(1)}, bf16[64,2816]{1,0:T(8,128)(2,1)S(1)}) custom-call(bf16[4,2,16,1024]{3,2,1,0:T(8,128)(2,1)S(1)} %pad_maximum_fusion.a_0_.a_4_.refs_8_.a_8_, bf16[4,2,16,1024]{3,2,1,0:T(8,128)(2,1)S(1)} %collective-permute-done.3.a_1_.a_5_.refs_9_.a_9_, ...), custom_call_target="tpu_custom_call" | custom-call | tf_op jit(solution)/shard_map/pallas_call | solution.py:49
  28.5 2.2 %collective-permute-done.15.a_2_.a_6_.refs_14_.a_14_ = bf16[4,2,16,1024]{3,2,1,0:T(8,128)(2,1)S(1)} collective-permute-done((bf16[4,2,16,1024]{3,2,1,0:T(8,128)(2,1)S(1)}, bf16[4,2,16,1024]{3,2,1,0:T(8,128)(2,1)S(1)}, u32[]{:S(2)}, u32[]{:S(2)}) %collective-permute-start.15) | collective-permute-done | bytes 262176 | tf_op jit(solution)/shard_map/ppermute | solution.py:28
  30.6 4.7 %collective-permute-done.13.a_0_.a_4_.refs_12_.a_12_ = bf16[4,2,16,1024]{3,2,1,0:T(8,128)(2,1)S(1)} collective-permute-done((bf16[4,2,16,1024]{3,2,1,0:T(8,128)(2,1)S(1)}, bf16[4,2,16,1024]{3,2,1,0:T(8,128)(2,1)S(1)}, u32[]{:S(2)}, u32[]{:S(2)}) %collective-permute-start.13) | collective-permute-done | bytes 262176 | tf_op jit(solution)/shard_map/ppermute | solution.py:28
  36.9 1.8 %shard_map.106 = (f32[64,2816]{1,0:T(8,128)S(1)}, bf16[64,2816]{1,0:T(8,128)(2,1)S(1)}, bf16[64,2816]{1,0:T(8,128)(2,1)S(1)}, bf16[64,2816]{1,0:T(8,128)(2,1)S(1)}) custom-call(bf16[4,2,16,1024]{3,2,1,0:T(8,128)(2,1)S(1)} %collective-permute-done.13.a_0_.a_4_.refs_12_.a_12_, bf16[4,2,16,1024]{3,2,1,0:T(8,128)(2,1)S(1)} %collective-permute-done.14.a_1_.a_5_.refs_13_.a_13_, ...), custom_call_target="tpu_custom_call" | custom-call | tf_op jit(solution)/shard_map/pallas_call | solution.py:49
  42.1 2.2 %collective-permute-done.7.b = bf16[64,2816]{1,0:T(8,128)(2,1)S(1)} collective-permute-done((bf16[64,2816]{1,0:T(8,128)(2,1)S(1)}, bf16[64,2816]{1,0:T(8,128)(2,1)S(1)}, u32[]{:S(2)}, u32[]{:S(2)}) %collective-permute-start.7) | collective-permute-done | bytes 360480 | tf_op jit(solution)/shard_map/ppermute | solution.py:28
  44.3 2.1 %collective-permute-done.8.c = bf16[64,2816]{1,0:T(8,128)(2,1)S(1)} collective-permute-done((bf16[64,2816]{1,0:T(8,128)(2,1)S(1)}, bf16[64,2816]{1,0:T(8,128)(2,1)S(1)}, u32[]{:S(2)}, u32[]{:S(2)}) %collective-permute-start.8) | collective-permute-done | bytes 360480 | tf_op jit(solution)/shard_map/ppermute | solution.py:28
  46.8 5.7 %collective-permute-start.9 = (bf16[64,2816]{1,0:T(8,128)(2,1)S(1)}, bf16[64,2816]{1,0:T(8,128)(2,1)S(1)}, u32[]{:S(2)}, u32[]{:S(2)}) collective-permute-start(bf16[64,2816]{1,0:T(8,128)(2,1)S(1)} %get-tuple-element.51), channel_id=1, source_target_pairs={{0,32},{32,0},{1,33},{33,1},{2,34},{34,2},{3,35},{35,3},{4,36},{36... | collective-permute-start | bytes 1081352 | tf_op jit(solution)/shard_map/ppermute | solution.py:28
  52.5 6.3 %collective-permute-done.18.b = bf16[64,2816]{1,0:T(8,128)(2,1)S(1)} collective-permute-done((bf16[64,2816]{1,0:T(8,128)(2,1)S(1)}, bf16[64,2816]{1,0:T(8,128)(2,1)S(1)}, u32[]{:S(2)}, u32[]{:S(2)}) %collective-permute-start.18) | collective-permute-done | bytes 360480 | tf_op jit(solution)/shard_map/ppermute | solution.py:28
  58.8 1.9 %collective-permute-done.19.c = bf16[64,2816]{1,0:T(8,128)(2,1)S(1)} collective-permute-done((bf16[64,2816]{1,0:T(8,128)(2,1)S(1)}, bf16[64,2816]{1,0:T(8,128)(2,1)S(1)}, u32[]{:S(2)}, u32[]{:S(2)}) %collective-permute-start.19) | collective-permute-done | bytes 360480 | tf_op jit(solution)/shard_map/ppermute | solution.py:28
  61.0 5.7 %collective-permute-start.20 = (bf16[64,2816]{1,0:T(8,128)(2,1)S(1)}, bf16[64,2816]{1,0:T(8,128)(2,1)S(1)}, u32[]{:S(2)}, u32[]{:S(2)}) collective-permute-start(bf16[64,2816]{1,0:T(8,128)(2,1)S(1)} %get-tuple-element.58), channel_id=1, source_target_pairs={{0,32},{32,0},{1,33},{33,1},{2,34},{34,2},{3,35},{35,3},{4,36},{36... | collective-permute-start | bytes 1081352 | tf_op jit(solution)/shard_map/ppermute | solution.py:28
  68.2 9.9 %collective-permute-start.11 = (bf16[64,2816]{1,0:T(8,128)(2,1)S(1)}, bf16[64,2816]{1,0:T(8,128)(2,1)S(1)}, u32[]{:S(2)}, u32[]{:S(2)}) collective-permute-start(bf16[64,2816]{1,0:T(8,128)(2,1)S(1)} %shard_map.104.a_0_.refs_0_), channel_id=1, source_target_pairs={{0,128},{64,192},{128,0},{192,64},{1,129},{65,193},{129,1},{193,65... | collective-permute-start | bytes 1081352 | tf_op jit(solution)/shard_map/ppermute | solution.py:28
  78.1 8.1 %collective-permute-done.20.other = bf16[64,2816]{1,0:T(8,128)(2,1)S(1)} collective-permute-done((bf16[64,2816]{1,0:T(8,128)(2,1)S(1)}, bf16[64,2816]{1,0:T(8,128)(2,1)S(1)}, u32[]{:S(2)}, u32[]{:S(2)}) %collective-permute-start.20) | collective-permute-done | bytes 360480 | tf_op jit(solution)/shard_map/ppermute | solution.py:28
  86.7 3.5 %collective-permute-start.23 = (bf16[64,2816]{1,0:T(8,128)(2,1)S(1)}, bf16[64,2816]{1,0:T(8,128)(2,1)S(1)}, u32[]{:S(2)}, u32[]{:S(2)}) collective-permute-start(bf16[64,2816]{1,0:T(8,128)(2,1)S(1)} %shard_map.108.a_0_.refs_4_.a_4_), channel_id=1, source_target_pairs={{0,64},{64,128},{128,192},{192,0},{1,65},{65,129},{129,193},{193,1... | collective-permute-start | bytes 1081352 | tf_op jit(solution)/shard_map/ppermute | solution.py:28
  93.1 11.7 %collective-permute-done.23.a_3_.refs_7_.a_7_ = bf16[64,2816]{1,0:T(8,128)(2,1)S(1)} collective-permute-done((bf16[64,2816]{1,0:T(8,128)(2,1)S(1)}, bf16[64,2816]{1,0:T(8,128)(2,1)S(1)}, u32[]{:S(2)}, u32[]{:S(2)}) %collective-permute-start.23) | collective-permute-done | bytes 360480 | tf_op jit(solution)/shard_map/ppermute | solution.py:28
  115.2 2.4 %shard_map.112 = bf16[896,1024]{1,0:T(8,128)(2,1)} custom-call(bf16[64,2816]{1,0:T(8,128)(2,1)S(1)} %shard_map.104.a_0_.refs_0_, bf16[64,2816]{1,0:T(8,128)(2,1)S(1)} %collective-permute-done.10.a_1_.refs_1_, bf16[64,2816]{1,0:T(8,128)(2,1)S(1)} %collective-permute-done.11.a_2_.refs_2_, bf16[64,2816]{1,0:T(8,128)(2,1)S(1)} %collective-permute-done.12.a_3_.refs_3_, ...), custom_call_target="tpu_custom_call" | custom-call | tf_op jit(solution)/shard_map/pallas_call | solution.py:49
  117.6 2.6 %shard_map.113 = bf16[1024,896]{1,0:T(8,128)(2,1)} custom-call(bf16[64,2816]{1,0:T(8,128)(2,1)S(1)} %shard_map.104.a_0_.refs_0_, bf16[64,2816]{1,0:T(8,128)(2,1)S(1)} %collective-permute-done.10.a_1_.refs_1_, bf16[64,2816]{1,0:T(8,128)(2,1)S(1)} %collective-permute-done.11.a_2_.refs_2_, bf16[64,2816]{1,0:T(8,128)(2,1)S(1)} %collective-permute-done.12.a_3_.refs_3_, ...), custom_call_target="tpu_custom_call" | custom-call | tf_op jit(solution)/shard_map/pallas_call | solution.py:49
  120.2 3.9 %collective-permute-done.27.refs_2_ = bf16[80,1152]{1,0:T(8,128)(2,1)S(1)} collective-permute-done((bf16[80,1152]{1,0:T(8,128)(2,1)S(1)}, bf16[80,1152]{1,0:T(8,128)(2,1)S(1)}, u32[]{:S(2)}, u32[]{:S(2)}) %collective-permute-start.27) | collective-permute-done | bytes 184352 | tf_op jit(solution)/shard_map/ppermute | solution.py:28
  124.5 3.7 %collective-permute-start.31 = (bf16[32,1152]{1,0:T(8,128)(2,1)S(1)}, bf16[32,1152]{1,0:T(8,128)(2,1)S(1)}, u32[]{:S(2)}, u32[]{:S(2)}) collective-permute-start(bf16[32,1152]{1,0:T(8,128)(2,1)S(1)} %get-tuple-element.76), channel_id=1, source_target_pairs={{0,6},{2,0},{4,2},{6,4},{1,7},{3,1},{5,3},{7,5},{8,14},{10,8},{12,... | collective-permute-start | bytes 221192 | tf_op jit(solution)/shard_map/ppermute | solution.py:28
  128.2 2.6 %shard_map.115 = bf16[1024,896]{1,0:T(8,128)(2,1)} custom-call(bf16[64,2816]{1,0:T(8,128)(2,1)S(1)} %shard_map.104.a_0_.refs_0_, bf16[64,2816]{1,0:T(8,128)(2,1)S(1)} %collective-permute-done.10.a_1_.refs_1_, bf16[64,2816]{1,0:T(8,128)(2,1)S(1)} %collective-permute-done.11.a_2_.refs_2_, bf16[64,2816]{1,0:T(8,128)(2,1)S(1)} %collective-permute-done.12.a_3_.refs_3_, ...), custom_call_target="tpu_custom_call" | custom-call | tf_op jit(solution)/shard_map/pallas_call | solution.py:49
  (62 shorter events, 34.2 us)
Async XLA Ops:
  12.3 8.1 %collective-permute-start.4 = (bf16[4,2,16,1024]{3,2,1,0:T(8,128)(2,1)S(1)}, bf16[4,2,16,1024]{3,2,1,0:T(8,128)(2,1)S(1)}, u32[]{:S(2)}, u32[]{:S(2)}) collective-permute-start(bf16[4,2,16,1024]{3,2,1,0:T(8,128)(2,1)S(1)} %pad_maximum_fusion.a_0_.a_4_.refs_8_.a_8_), channel_id=1, source_target_pairs={{0,8},{8,16},{16,24},{24,0},{1,9},{9,17},{17,25},{25,1},{2,10},{10... | collective-permute-start | bytes 786440 | tf_op jit(solution)/shard_map/ppermute | solution.py:28
  16.6 6.8 %collective-permute-start.3 = (bf16[4,2,16,1024]{3,2,1,0:T(8,128)(2,1)S(1)}, bf16[4,2,16,1024]{3,2,1,0:T(8,128)(2,1)S(1)}, u32[]{:S(2)}, u32[]{:S(2)}) collective-permute-start(bf16[4,2,16,1024]{3,2,1,0:T(8,128)(2,1)S(1)} %pad_maximum_fusion.a_0_.a_4_.refs_8_.a_8_), channel_id=1, source_target_pairs={{0,1},{1,0},{2,3},{3,2},{4,5},{5,4},{6,7},{7,6},{8,9},{9,8},{10,11... | collective-permute-start | bytes 786440 | tf_op jit(solution)/shard_map/ppermute | solution.py:28
  20.4 10.2 %collective-permute-start.15 = (bf16[4,2,16,1024]{3,2,1,0:T(8,128)(2,1)S(1)}, bf16[4,2,16,1024]{3,2,1,0:T(8,128)(2,1)S(1)}, u32[]{:S(2)}, u32[]{:S(2)}) collective-permute-start(bf16[4,2,16,1024]{3,2,1,0:T(8,128)(2,1)S(1)} %pad_maximum_fusion.a_0_.a_4_.refs_8_.a_8_), channel_id=1, source_target_pairs={{0,16},{8,24},{16,0},{24,8},{1,17},{9,25},{17,1},{25,9},{2,18},{10... | collective-permute-start | bytes 786440 | tf_op jit(solution)/shard_map/ppermute | solution.py:28
  22.3 13.0 %collective-permute-start.13 = (bf16[4,2,16,1024]{3,2,1,0:T(8,128)(2,1)S(1)}, bf16[4,2,16,1024]{3,2,1,0:T(8,128)(2,1)S(1)}, u32[]{:S(2)}, u32[]{:S(2)}) collective-permute-start(bf16[4,2,16,1024]{3,2,1,0:T(8,128)(2,1)S(1)} %pad_maximum_fusion.a_0_.a_4_.refs_8_.a_8_), channel_id=1, source_target_pairs={{0,24},{8,0},{16,8},{24,16},{1,25},{9,1},{17,9},{25,17},{2,26},{10... | collective-permute-start | bytes 786440 | tf_op jit(solution)/shard_map/ppermute | solution.py:28
  25.2 15.8 %collective-permute-start.6 = (bf16[64,2816]{1,0:T(8,128)(2,1)S(1)}, bf16[64,2816]{1,0:T(8,128)(2,1)S(1)}, u32[]{:S(2)}, u32[]{:S(2)}) collective-permute-start(bf16[64,2816]{1,0:T(8,128)(2,1)S(1)} %get-tuple-element.47), channel_id=1, source_target_pairs={{0,64},{64,128},{128,192},{192,0},{1,65},{65,129},{129,193},{193,1... | collective-permute-start | bytes 1081352 | tf_op jit(solution)/shard_map/ppermute | solution.py:28
  26.5 17.8 %collective-permute-start.7 = (bf16[64,2816]{1,0:T(8,128)(2,1)S(1)}, bf16[64,2816]{1,0:T(8,128)(2,1)S(1)}, u32[]{:S(2)}, u32[]{:S(2)}) collective-permute-start(bf16[64,2816]{1,0:T(8,128)(2,1)S(1)} %get-tuple-element.48), channel_id=1, source_target_pairs={{0,128},{64,192},{128,0},{192,64},{1,129},{65,193},{129,1},{193,65... | collective-permute-start | bytes 1081352 | tf_op jit(solution)/shard_map/ppermute | solution.py:28
  27.3 19.1 %collective-permute-start.8 = (bf16[64,2816]{1,0:T(8,128)(2,1)S(1)}, bf16[64,2816]{1,0:T(8,128)(2,1)S(1)}, u32[]{:S(2)}, u32[]{:S(2)}) collective-permute-start(bf16[64,2816]{1,0:T(8,128)(2,1)S(1)} %get-tuple-element.49), channel_id=1, source_target_pairs={{0,192},{64,0},{128,64},{192,128},{1,193},{65,1},{129,65},{193,129... | collective-permute-start | bytes 1081352 | tf_op jit(solution)/shard_map/ppermute | solution.py:28
  38.7 13.8 %collective-permute-start.17 = (bf16[64,2816]{1,0:T(8,128)(2,1)S(1)}, bf16[64,2816]{1,0:T(8,128)(2,1)S(1)}, u32[]{:S(2)}, u32[]{:S(2)}) collective-permute-start(bf16[64,2816]{1,0:T(8,128)(2,1)S(1)} %get-tuple-element.54), channel_id=1, source_target_pairs={{0,64},{64,128},{128,192},{192,0},{1,65},{65,129},{129,193},{193,1... | collective-permute-start | bytes 1081352 | tf_op jit(solution)/shard_map/ppermute | solution.py:28
  40.2 18.6 %collective-permute-start.18 = (bf16[64,2816]{1,0:T(8,128)(2,1)S(1)}, bf16[64,2816]{1,0:T(8,128)(2,1)S(1)}, u32[]{:S(2)}, u32[]{:S(2)}) collective-permute-start(bf16[64,2816]{1,0:T(8,128)(2,1)S(1)} %get-tuple-element.55), channel_id=1, source_target_pairs={{0,128},{64,192},{128,0},{192,64},{1,129},{65,193},{129,1},{193,65... | collective-permute-start | bytes 1081352 | tf_op jit(solution)/shard_map/ppermute | solution.py:28
  41.0 19.6 %collective-permute-start.19 = (bf16[64,2816]{1,0:T(8,128)(2,1)S(1)}, bf16[64,2816]{1,0:T(8,128)(2,1)S(1)}, u32[]{:S(2)}, u32[]{:S(2)}) collective-permute-start(bf16[64,2816]{1,0:T(8,128)(2,1)S(1)} %get-tuple-element.56), channel_id=1, source_target_pairs={{0,192},{64,0},{128,64},{192,128},{1,193},{65,1},{129,65},{193,129... | collective-permute-start | bytes 1081352 | tf_op jit(solution)/shard_map/ppermute | solution.py:28
  46.8 19.9 %collective-permute-start.9 = (bf16[64,2816]{1,0:T(8,128)(2,1)S(1)}, bf16[64,2816]{1,0:T(8,128)(2,1)S(1)}, u32[]{:S(2)}, u32[]{:S(2)}) collective-permute-start(bf16[64,2816]{1,0:T(8,128)(2,1)S(1)} %get-tuple-element.51), channel_id=1, source_target_pairs={{0,32},{32,0},{1,33},{33,1},{2,34},{34,2},{3,35},{35,3},{4,36},{36... | collective-permute-start | bytes 1081352 | tf_op jit(solution)/shard_map/ppermute | solution.py:28
  61.0 25.2 %collective-permute-start.20 = (bf16[64,2816]{1,0:T(8,128)(2,1)S(1)}, bf16[64,2816]{1,0:T(8,128)(2,1)S(1)}, u32[]{:S(2)}, u32[]{:S(2)}) collective-permute-start(bf16[64,2816]{1,0:T(8,128)(2,1)S(1)} %get-tuple-element.58), channel_id=1, source_target_pairs={{0,32},{32,0},{1,33},{33,1},{2,34},{34,2},{3,35},{35,3},{4,36},{36... | collective-permute-start | bytes 1081352 | tf_op jit(solution)/shard_map/ppermute | solution.py:28
  67.1 23.1 %collective-permute-start.12 = (bf16[64,2816]{1,0:T(8,128)(2,1)S(1)}, bf16[64,2816]{1,0:T(8,128)(2,1)S(1)}, u32[]{:S(2)}, u32[]{:S(2)}) collective-permute-start(bf16[64,2816]{1,0:T(8,128)(2,1)S(1)} %shard_map.104.a_0_.refs_0_), channel_id=1, source_target_pairs={{0,64},{64,128},{128,192},{192,0},{1,65},{65,129},{129,193},{193,1... | collective-permute-start | bytes 1081352 | tf_op jit(solution)/shard_map/ppermute | solution.py:28
  68.2 23.6 %collective-permute-start.11 = (bf16[64,2816]{1,0:T(8,128)(2,1)S(1)}, bf16[64,2816]{1,0:T(8,128)(2,1)S(1)}, u32[]{:S(2)}, u32[]{:S(2)}) collective-permute-start(bf16[64,2816]{1,0:T(8,128)(2,1)S(1)} %shard_map.104.a_0_.refs_0_), channel_id=1, source_target_pairs={{0,128},{64,192},{128,0},{192,64},{1,129},{65,193},{129,1},{193,65... | collective-permute-start | bytes 1081352 | tf_op jit(solution)/shard_map/ppermute | solution.py:28
  78.1 13.7 %collective-permute-start.10 = (bf16[64,2816]{1,0:T(8,128)(2,1)S(1)}, bf16[64,2816]{1,0:T(8,128)(2,1)S(1)}, u32[]{:S(2)}, u32[]{:S(2)}) collective-permute-start(bf16[64,2816]{1,0:T(8,128)(2,1)S(1)} %shard_map.104.a_0_.refs_0_), channel_id=1, source_target_pairs={{0,192},{64,0},{128,64},{192,128},{1,193},{65,1},{129,65},{193,129... | collective-permute-start | bytes 1081352 | tf_op jit(solution)/shard_map/ppermute | solution.py:28
  86.7 18.1 %collective-permute-start.23 = (bf16[64,2816]{1,0:T(8,128)(2,1)S(1)}, bf16[64,2816]{1,0:T(8,128)(2,1)S(1)}, u32[]{:S(2)}, u32[]{:S(2)}) collective-permute-start(bf16[64,2816]{1,0:T(8,128)(2,1)S(1)} %shard_map.108.a_0_.refs_4_.a_4_), channel_id=1, source_target_pairs={{0,64},{64,128},{128,192},{192,0},{1,65},{65,129},{129,193},{193,1... | collective-permute-start | bytes 1081352 | tf_op jit(solution)/shard_map/ppermute | solution.py:28
  90.2 15.6 %collective-permute-start.22 = (bf16[64,2816]{1,0:T(8,128)(2,1)S(1)}, bf16[64,2816]{1,0:T(8,128)(2,1)S(1)}, u32[]{:S(2)}, u32[]{:S(2)}) collective-permute-start(bf16[64,2816]{1,0:T(8,128)(2,1)S(1)} %shard_map.108.a_0_.refs_4_.a_4_), channel_id=1, source_target_pairs={{0,128},{64,192},{128,0},{192,64},{1,129},{65,193},{129,1},{193,65... | collective-permute-start | bytes 1081352 | tf_op jit(solution)/shard_map/ppermute | solution.py:28
  90.2 16.5 %collective-permute-start.21 = (bf16[64,2816]{1,0:T(8,128)(2,1)S(1)}, bf16[64,2816]{1,0:T(8,128)(2,1)S(1)}, u32[]{:S(2)}, u32[]{:S(2)}) collective-permute-start(bf16[64,2816]{1,0:T(8,128)(2,1)S(1)} %shard_map.108.a_0_.refs_4_.a_4_), channel_id=1, source_target_pairs={{0,192},{64,0},{128,64},{192,128},{1,193},{65,1},{129,65},{193,129... | collective-permute-start | bytes 1081352 | tf_op jit(solution)/shard_map/ppermute | solution.py:28
  111.4 8.8 %collective-permute-start.26 = (bf16[80,1152]{1,0:T(8,128)(2,1)S(1)}, bf16[80,1152]{1,0:T(8,128)(2,1)S(1)}, u32[]{:S(2)}, u32[]{:S(2)}) collective-permute-start(bf16[80,1152]{1,0:T(8,128)(2,1)S(1)} %get-tuple-element.65), channel_id=1, source_target_pairs={{0,24},{8,0},{16,8},{24,16},{1,25},{9,1},{17,9},{25,17},{2,26},{10... | collective-permute-start | bytes 552968 | tf_op jit(solution)/shard_map/ppermute | solution.py:28
  112.5 11.6 %collective-permute-start.27 = (bf16[80,1152]{1,0:T(8,128)(2,1)S(1)}, bf16[80,1152]{1,0:T(8,128)(2,1)S(1)}, u32[]{:S(2)}, u32[]{:S(2)}) collective-permute-start(bf16[80,1152]{1,0:T(8,128)(2,1)S(1)} %get-tuple-element.66), channel_id=1, source_target_pairs={{0,8},{8,16},{16,24},{24,0},{1,9},{9,17},{17,25},{25,1},{2,10},{10... | collective-permute-start | bytes 552968 | tf_op jit(solution)/shard_map/ppermute | solution.py:28
  113.5 10.6 %collective-permute-start.28 = (bf16[80,1152]{1,0:T(8,128)(2,1)S(1)}, bf16[80,1152]{1,0:T(8,128)(2,1)S(1)}, u32[]{:S(2)}, u32[]{:S(2)}) collective-permute-start(bf16[80,1152]{1,0:T(8,128)(2,1)S(1)} %get-tuple-element.67), channel_id=1, source_target_pairs={{0,16},{8,24},{16,0},{24,8},{1,17},{9,25},{17,1},{25,9},{2,18},{10... | collective-permute-start | bytes 552968 | tf_op jit(solution)/shard_map/ppermute | solution.py:28
  124.3 6.5 %collective-permute-start.29 = (bf16[32,1152]{1,0:T(8,128)(2,1)S(1)}, bf16[32,1152]{1,0:T(8,128)(2,1)S(1)}, u32[]{:S(2)}, u32[]{:S(2)}) collective-permute-start(bf16[32,1152]{1,0:T(8,128)(2,1)S(1)} %get-tuple-element.72), channel_id=1, source_target_pairs={{0,2},{2,4},{4,6},{6,0},{1,3},{3,5},{5,7},{7,1},{8,10},{10,12},{12... | collective-permute-start | bytes 221192 | tf_op jit(solution)/shard_map/ppermute | solution.py:28
  124.4 7.5 %collective-permute-start.30 = (bf16[32,1152]{1,0:T(8,128)(2,1)S(1)}, bf16[32,1152]{1,0:T(8,128)(2,1)S(1)}, u32[]{:S(2)}, u32[]{:S(2)}) collective-permute-start(bf16[32,1152]{1,0:T(8,128)(2,1)S(1)} %get-tuple-element.74), channel_id=1, source_target_pairs={{0,4},{2,6},{4,0},{6,2},{1,5},{3,7},{5,1},{7,3},{8,12},{10,14},{12... | collective-permute-start | bytes 221192 | tf_op jit(solution)/shard_map/ppermute | solution.py:28
  124.5 7.4 %collective-permute-start.31 = (bf16[32,1152]{1,0:T(8,128)(2,1)S(1)}, bf16[32,1152]{1,0:T(8,128)(2,1)S(1)}, u32[]{:S(2)}, u32[]{:S(2)}) collective-permute-start(bf16[32,1152]{1,0:T(8,128)(2,1)S(1)} %get-tuple-element.76), channel_id=1, source_target_pairs={{0,6},{2,0},{4,2},{6,4},{1,7},{3,1},{5,3},{7,5},{8,14},{10,8},{12,... | collective-permute-start | bytes 221192 | tf_op jit(solution)/shard_map/ppermute | solution.py:28
  (10 other events, 49.8 us)

commit v2 on v1

--- a/solution.py
+++ b/solution.py
@@ -15,7 +15,6 @@
 CONTRACT_FIRST = (((0,), (0,)), ((), ()))
 STEPS = (0, 1, -1, 2)
 PARTS = 4
-EXTRA = 16
 GROUPS = ((0, 1), (2, 3))
 GAINS = GROUPS[-1]
 
@@ -45,7 +44,7 @@
     return block[:, at : at + 1] + block[:, at + 1 : at + 2] + block[:, at + 2 : at + 3]
 
 
-def call(kernel, out_shapes, args, limit=24, flops=0):
+def call(kernel, out_shapes, args, limit=24):
     return pl.pallas_call(
         kernel,
         out_shape=[jax.ShapeDtypeStruct(s, d) for s, d in out_shapes],
@@ -80,19 +79,27 @@
     )(*[pltpu.with_memory_space_constraint(w, pltpu.HBM) for w in weights])
 
 
-def split(row):
-    line = lax.broadcasted_iota(jnp.int32, (EXTRA, row.shape[1]), 0)
-    out = jnp.zeros((EXTRA, row.shape[1]), F32)
-    for at in range(3):
-        piece = row.astype(BF).astype(F32)
-        out = jnp.where(line == at, piece, out)
-        row = row - piece
-    return out.astype(BF)
-
-
-def joined(block):
-    block = block.astype(F32)
-    return block[0:1] + block[1:2] + block[2:3]
+def pack(row, rows):
+    pieces = []
+    for _ in range(3):
+        pieces.append(row.astype(BF).astype(F32))
+        row = row - pieces[-1]
+    cuts = row.shape[1] // LANES
+    line = lax.broadcasted_iota(jnp.int32, (rows, LANES), 0)
+    tiles = [jnp.zeros((rows, LANES), F32) for _ in range(-(-3 * cuts // rows))]
+    for at in range(3 * cuts):
+        piece = pieces[at // cuts][:, at % cuts * LANES : at % cuts * LANES + LANES]
+        tiles[at // rows] = jnp.where(line == at % rows, piece, tiles[at // rows])
+    return jnp.concatenate(tiles, axis=1).astype(BF)
+
+
+def unpack(block, width):
+    block, rows, cuts = block.astype(F32), block.shape[0], width // LANES
+    cut = [
+        block[at % rows : at % rows + 1, at // rows * LANES : at // rows * LANES + LANES]
+        for at in range(3 * cuts)
+    ]
+    return sum(jnp.concatenate(cut[p * cuts : p * cuts + cuts], axis=1) for p in range(3))
 
 
 def label(slot):
@@ -139,7 +146,7 @@
     out[...] = value.astype(BF)
 
 
-def activate(own, other, out):
+def activate(own, other, out, hidden=None):
     total = own[...] + other[...].astype(F32)
     width = (total.shape[1] - LANES) // 3
     inv = lax.rsqrt(head(total[:, -LANES:], 0) / D + 1e-05)
@@ -153,8 +160,11 @@
     mean = jnp.sum(d_gate * gate + d_up * up, axis=1, keepdims=True)
     out[:, :width] = d_gate.astype(BF)
     out[:, width : 2 * width] = d_up.astype(BF)
-    out[:, 2 * width : 3 * width] = (silu * up).astype(BF)
-    out[:, 3 * width :] = tail(inv, mean).astype(BF)
+    out[:, 2 * width : 2 * width + LANES] = tail(inv, mean).astype(BF)
+    if hidden is None:
+        out[:, 2 * width + LANES :] = (silu * up).astype(BF)
+    else:
+        hidden[...] = (silu * up).astype(BF)
 
 
 def backward(size, *refs):
@@ -170,7 +180,7 @@
     ) + lax.dot_general(
         rows_of(width, 2 * width), up_w[...], CONTRACT_LAST, preferred_element_type=F32
     )
-    end = rows_of(3 * width, 3 * width + LANES).astype(F32)
+    end = rows_of(2 * width, 2 * width + LANES).astype(F32)
     inv = head(end, 0)
     mean = tail(head(end, 3))
     x = tokens(blocks, 0).astype(F32)
@@ -194,68 +204,80 @@
     mine, received, gains, outs = refs[:count], refs[count : 2 * count], refs[-5], refs[-4:]
     depth = gains.shape[1]
     last = 64 * len(GROUPS[-1])
-    gain = gains[...] + received[-1][last : last + 1, :depth]
+    packed = pack(gains[...] + received[-1][last : last + 1, :depth], 64)
     for g, group in enumerate(GROUPS):
         for i, block in enumerate(group):
             rows = slice(64 * i, 64 * i + 64)
             value, out = mine[g][rows] + received[g][rows], outs[block]
-            out[:64, :depth] = value[:, :depth].astype(BF)
-            out[:64, depth:] = tail(head(value[:, depth:], 0)).astype(BF)
-            out[64:, :depth] = split(gain)
-            out[64:, depth:] = jnp.zeros((EXTRA, LANES), BF)
+            out[:, :depth] = value[:, :depth].astype(BF)
+            out[:, depth : depth + LANES] = tail(head(value[:, depth:], 0)).astype(BF)
+            out[:, depth + LANES :] = packed
 
 
 def add_y(*refs):
-    parts, outs = refs[:4], refs[4:]
-    depth = parts[0].shape[1] - LANES
-    total = sum(p[:64].astype(F32) for p in parts)
-    gain = sum(joined(p[64:, :depth]) for p in parts)
-    outs[0][:16] = total[:16]
-    outs[0][16:, :depth] = jnp.broadcast_to(gain, (EXTRA, depth))
-    outs[0][16:, depth:] = jnp.zeros((EXTRA, LANES), F32)
+    parts, gain_out, outs = refs[:4], refs[4], refs[5:]
+    depth = gain_out.shape[1]
+    deep = depth + LANES
+    total = sum(p[:, :deep].astype(F32) for p in parts)
+    gain = sum(unpack(p[:, deep:], depth) for p in parts)
+    gain_out[...] = gain
+    outs[0][...] = total[:16]
+    packed = pack(gain, 16)
     for s in range(1, 4):
-        outs[s][:16, :depth] = total[16 * s : 16 * s + 16, :depth].astype(BF)
-        outs[s][:16, depth:] = tail(head(total[16 * s : 16 * s + 16, depth:], 0)).astype(BF)
-        outs[s][16:, :depth] = split(gain)
-        outs[s][16:, depth:] = jnp.zeros((EXTRA, LANES), BF)
-
-
-def finish(own, a, b, c, x, inv, gain, grad_input, grad_gain):
+        outs[s][:, :depth] = total[16 * s : 16 * s + 16, :depth].astype(BF)
+        outs[s][:, depth:deep] = tail(head(total[16 * s : 16 * s + 16, depth:], 0)).astype(BF)
+        outs[s][:, deep:] = packed
+
+
+def finish(own, a, b, c, own_gain, x, inv, gain, grad_input, grad_gain):
     depth = x.shape[1]
-    total = own[:16] + sum(v[:16].astype(F32) for v in (a, b, c))
+    deep = depth + LANES
+    total = own[...] + sum(v[:, :deep].astype(F32) for v in (a, b, c))
     inv = inv[0, :16]
     mean = head(total[:, depth:], 0) / D
-    grad_gain[...] = own[16:17, :depth] + sum(joined(v[16:, :depth]) for v in (a, b, c))
+    grad_gain[...] = own_gain[...] + sum(unpack(v[:, deep:], depth) for v in (a, b, c))
     grad_input[...] = (
         inv * total[:, :depth] * gain[...] - x[...].astype(F32) * inv * inv * mean
     ).astype(BF)
 
 
-def wide_grads(at, *refs):
-    count = len(GROUPS)
-    messages, blocks = refs[: 4 * count], pairs(refs[4 * count : 4 * count + 8])
-    invs, (gain, out) = refs[4 * count + 8 : -2], refs[-2:]
+def operands(group, refs):
+    blocks, inv, gain = pairs(refs[4:-2]), refs[-2], refs[-1]
+    inv = jnp.concatenate([inv[label(s)] for s in range(4)], axis=0)
+    normed = (tokens(blocks, 0).astype(F32) * inv * gain[...]).astype(BF)
+    return normed, tokens(blocks, 1)
+
+
+def product(left, right):
+    return lax.dot_general(left, right, CONTRACT_FIRST, preferred_element_type=F32)
+
+
+def columns(messages, start, stop):
+    return jnp.concatenate([m[:, start:stop] for m in messages], axis=0)
+
+
+def early_grads(group, *refs):
+    refs, outs = refs[:-3], refs[-3:]
+    normed, grad = operands(group, refs)
+    width = outs[0].shape[1]
+    top = refs[0].shape[1]
+    for at in (0, 1):
+        outs[at][...] = product(normed, columns(refs[:4], at * width, at * width + width))
+    outs[2][...] = product(columns(refs[:4], top - width, top), grad)
+
+
+def wide_grads(at, group, *refs):
+    refs, total, out = refs[:-2], refs[-2], refs[-1]
+    normed, _ = operands(group, refs)
     width = out.shape[1]
-    normed = []
-    for g, group in enumerate(GROUPS):
-        members = [blocks[i] for i in group]
-        inv = jnp.concatenate([invs[g][label(s)] for s in range(4)], axis=0)
-        normed.append((tokens(members, 0).astype(F32) * inv * gain[...]).astype(BF))
-    columns = jnp.concatenate([m[:, at * width : at * width + width] for m in messages], axis=0)
-    out[...] = lax.dot_general(
-        jnp.concatenate(normed, axis=0), columns, CONTRACT_FIRST, preferred_element_type=F32
-    ).astype(BF)
-
-
-def down_grads(*refs):
-    count = len(GROUPS)
-    messages, blocks, out = refs[: 4 * count], pairs(refs[4 * count : -1]), refs[-1]
-    width = out.shape[0]
-    grads = jnp.concatenate([tokens([blocks[i] for i in g], 1) for g in GROUPS], axis=0)
-    hidden = jnp.concatenate([m[:, 2 * width : 3 * width] for m in messages], axis=0)
-    out[...] = lax.dot_general(
-        hidden, grads, CONTRACT_FIRST, preferred_element_type=F32
-    ).astype(BF)
+    part = product(normed, columns(refs[:4], at * width, at * width + width))
+    out[...] = (total[...] + part).astype(BF)
+
+
+def down_grads(group, *refs):
+    hidden, blocks, total, out = refs[:4], pairs(refs[4:-2]), refs[-2], refs[-1]
+    part = product(jnp.concatenate([h[...] for h in hidden], axis=0), tokens(blocks, 1))
+    out[...] = (total[...] + part).astype(BF)
 
 
 def after(value, *earlier):
@@ -278,7 +300,6 @@
     def members(group):
         return [v for i in group for v in (own[i], other[i])]
 
-    unit = 2 * depth * width * 128
     totals, crossed = [], []
     for group in GROUPS:
         tall = 32 * len(group)
@@ -286,7 +307,6 @@
             lambda *a, n=len(group): forward(n, *a),
             [((tall, wide), F32)] + [((tall, wide), BF)] * 3,
             [*members(group), gain, gate_w, up_w, down_w],
-            flops=3 * unit * len(group),
         )
         total, out = call(
             add_x,
@@ -301,48 +321,65 @@
     for group, total, arrived in zip(GROUPS, totals, crossed):
         size = len(group)
         tall = 32 * size
-        (m0,) = call(activate, [((tall, wide), BF)], [total, arrived])
+        if len(invs) < len(GROUPS) - 1:
+            shapes = [((tall, wide), BF)]
+        else:
+            shapes = [((tall, 2 * width + LANES), BF), ((tall, width), BF)]
+        m0, *hidden = call(activate, shapes, [total, arrived])
         found = [m0, send(m0, "x", -1), send(m0, "x", 2), send(m0, "x", 1)]
         mine, theirs, inv, gains = call(
             lambda *a, n=size: backward(n, *a),
             [((64 * size, deep), F32), ((64 * size + 8, deep), F32), ((4, tall, 1), F32)]
             + [((1, depth), F32)],
             [*found, *members(group), gate_w, up_w, gains],
-            flops=2 * unit * size,
         )
-        halves.append((mine, send(theirs, "core", 1)))
+        received = send(theirs, "core", 1)
+        halves.append((mine, received))
+        if not messages:
+            early = call(
+                lambda *a: early_grads(group, *a),
+                [((depth, width), F32)] * 2 + [((width, depth), F32)],
+                [*found, *members(group), inv, gain],
+                limit=32,
+            )
+            gains = after(gains, *early)
         messages += found
         invs.append(inv)
 
     parts = call(
         add_core,
-        [((64 + EXTRA, deep), BF)] * 4,
+        [((64, deep + LANES), BF)] * 4,
         [*[h[0] for h in halves], *[h[1] for h in halves], gains],
     )
     parts = [parts[0]] + [send(parts[i], "y", -STEPS[i]) for i in (1, 2, 3)]
-    outs = call(
-        add_y, [((16 + EXTRA, deep), F32)] + [((16 + EXTRA, deep), BF)] * 3, parts
-    )
-    flat = [v for pair in zip(own, other) for v in pair]
+    gain_sum, *outs = call(
+        add_y,
+        [((1, depth), F32), ((16, deep), F32)] + [((16, deep + 2 * LANES), BF)] * 3,
+        parts,
+    )
+    hidden = after(hidden[0], *found[1:])
+    units = [hidden] + [send(hidden, "x", s) for s in (-1, 2, 1)]
     (grad_down,) = call(
-        down_grads, [((width, depth), BF)], [*messages, *flat], limit=32, flops=4 * unit
+        lambda *a: down_grads(group, *a),
+        [((width, depth), BF)],
+        [*units, *members(group), early[2]],
+        limit=32,
     )
     grad_gate, grad_up = (
         call(
-            lambda *a, n=at: wide_grads(n, *a),
+            lambda *a, n=at: wide_grads(n, group, *a),
             [((depth, width), BF)],
-            [*messages, *flat, *invs, gain],
+            [*found, *members(group), inv, gain, early[at]],
             limit=32,
-            flops=4 * unit,
         )[0]
         for at in (0, 1)
     )
     home_sums = [outs[0]]
-    home_sums += [send(after(outs[k], grad_down, grad_up), "zl", k) for k in (1, 2, 3)]
+    home_sums += [send(after(outs[k], grad_up, grad_gate), "zl", k) for k in (1, 2, 3)]
     grad_input, grad_gain = call(
         finish,
         [((rows, depth), BF), ((1, depth), F32)],
-        [*home_sums, activations, invs[0], gain],
+        [*home_sums, gain_sum, activations, invs[0], gain],
     )
     return (grad_input, grad_gain[0], grad_gate, grad_up, grad_down)
 

time: 135 us -> 130 us (0.963); the launches traced: 133 us -> 130 us
  waiting for transfers between devices: 59.2 us -> 47.6 us
  starting transfers between devices: 52.4 us -> 60.8 us
    ppermute x32 -> x35, waiting for transfers between devices: 59.2 us -> 47.6 us  [send(): lax.ppermute(value, axis, ring(2 if axis in ('zh', 'core') else 4, step))]
    ppermute x32 -> x35, starting transfers between devices: 52.4 us -> 60.8 us  [send(): lax.ppermute(value, axis, ring(2 if axis in ('zh', 'core') else 4, step))]
    pallas_call x14 -> x15, Pallas kernels: 16.8 us -> 17.2 us  [call(): pl.pallas_call(kernel, out_shape=[jax.ShapeDtypeStruct(s, d) for s, d in...]
  transfers between devices with their start and end apart: 32 -> 35, of which waited for: 19 -> 19; matrix products, arithmetic and copies ran while one was open for 0% -> 0% of each run, Pallas kernels for 13% -> 14%
where the time goes in v2:
time: 130 us
  starting transfers between devices  60.8 us (47%)
  waiting for transfers between devices  47.6 us (37%)
  Pallas kernels  19.8 us (15%)
    ppermute x35, starting transfers between devices, send(): lax.ppermute(value, axis, ring(2 if axis in ('zh', 'core') else 4, step))  60.8 us
    ppermute x35, waiting for transfers between devices, send(): lax.ppermute(value, axis, ring(2 if axis in ('zh', 'core') else 4, step))  47.6 us
    pallas_call x15, Pallas kernels, call(): pl.pallas_call(kernel, out_shape=[jax.ShapeDtypeStruct(s, d) for s, d in...  17.2 us
    pallas_call x1, Pallas kernels, load(): pl.pallas_call(kernel, out_shape=[jax.ShapeDtypeStruct(w.shape, w.dtype)...  2.64 us
  transfers between devices with their start and end apart: 35, of which 19 were waited for; matrix products, arithmetic and copies ran while one was open for 0% of the time, Pallas kernels for 14%

profile of v2, /device:TPU:4, one launch (start us, length us, event | category | flops | bytes accessed | tf_op | source)
XLA Modules:
  0.0 129.8 jit_solution(15908052994445754618)
XLA Ops:
  1.4 2.0 %collective-permute-start.2 = (bf16[2,16,1024]{2,1,0:T(8,128)(2,1)S(1)}, bf16[2,16,1024]{2,1,0:T(8,128)(2,1)S(1)}, u32[]{:S(2)}, u32[]{:S(2)}) collective-permute-start(bf16[2,16,1024]{2,1,0:T(8,128)(2,1)S(1)} %get-tuple-element.96), channel_id=1, source_target_pairs={{0,2},{2,4},{4,6},{6,0},{1,3},{3,5},{5,7},{7,1},{8,10},{10,12},{12... | collective-permute-start | bytes 196616 | tf_op jit(solution)/shard_map/ppermute | solution.py:27
  3.4 3.3 %collective-permute-start.1 = (bf16[2,16,1024]{2,1,0:T(8,128)(2,1)S(1)}, bf16[2,16,1024]{2,1,0:T(8,128)(2,1)S(1)}, u32[]{:S(2)}, u32[]{:S(2)}) collective-permute-start(bf16[2,16,1024]{2,1,0:T(8,128)(2,1)S(1)} %get-tuple-element.96), channel_id=1, source_target_pairs={{0,4},{2,6},{4,0},{6,2},{1,5},{3,7},{5,1},{7,3},{8,12},{10,14},{12... | collective-permute-start | bytes 196616 | tf_op jit(solution)/shard_map/ppermute | solution.py:27
  8.9 2.3 %collective-permute-done.1 = bf16[2,16,1024]{2,1,0:T(8,128)(2,1)S(1)} collective-permute-done((bf16[2,16,1024]{2,1,0:T(8,128)(2,1)S(1)}, bf16[2,16,1024]{2,1,0:T(8,128)(2,1)S(1)}, u32[]{:S(2)}, u32[]{:S(2)}) %collective-permute-start.1) | collective-permute-done | bytes 65568 | tf_op jit(solution)/shard_map/ppermute | solution.py:27
  13.2 2.6 %shard_map.101 = (bf16[1024,896]{1,0:T(8,128)(2,1)S(1)}, bf16[1024,896]{1,0:T(8,128)(2,1)S(1)}, bf16[896,1024]{1,0:T(8,128)(2,1)S(1)}) custom-call(bf16[1024,896]{1,0:T(8,128)(2,1)} %refs_0_.1, bf16[1024,896]{1,0:T(8,128)(2,1)} %refs_1_.1, bf16[896,1024]{1,0:T(8,128)(2,1)} %refs_2_.1), custom_call_target="tpu_custom_call" | custom-call | tf_op jit(solution)/shard_map/pallas_call | solution.py:72
  16.0 4.6 %collective-permute-done.4.a_2_.a_6_ = bf16[4,2,16,1024]{3,2,1,0:T(8,128)(2,1)S(1)} collective-permute-done((bf16[4,2,16,1024]{3,2,1,0:T(8,128)(2,1)S(1)}, bf16[4,2,16,1024]{3,2,1,0:T(8,128)(2,1)S(1)}, u32[]{:S(2)}, u32[]{:S(2)}) %collective-permute-start.4) | collective-permute-done | bytes 262176 | tf_op jit(solution)/shard_map/ppermute | solution.py:27
  29.7 2.6 %collective-permute-done.15.a_2_.a_6_ = bf16[4,2,16,1024]{3,2,1,0:T(8,128)(2,1)S(1)} collective-permute-done((bf16[4,2,16,1024]{3,2,1,0:T(8,128)(2,1)S(1)}, bf16[4,2,16,1024]{3,2,1,0:T(8,128)(2,1)S(1)}, u32[]{:S(2)}, u32[]{:S(2)}) %collective-permute-start.15) | collective-permute-done | bytes 262176 | tf_op jit(solution)/shard_map/ppermute | solution.py:27
  39.1 4.9 %collective-permute-done.7.b = bf16[64,2816]{1,0:T(8,128)(2,1)S(1)} collective-permute-done((bf16[64,2816]{1,0:T(8,128)(2,1)S(1)}, bf16[64,2816]{1,0:T(8,128)(2,1)S(1)}, u32[]{:S(2)}, u32[]{:S(2)}) %collective-permute-start.7) | collective-permute-done | bytes 360480 | tf_op jit(solution)/shard_map/ppermute | solution.py:27
  43.9 2.1 %collective-permute-done.8.c = bf16[64,2816]{1,0:T(8,128)(2,1)S(1)} collective-permute-done((bf16[64,2816]{1,0:T(8,128)(2,1)S(1)}, bf16[64,2816]{1,0:T(8,128)(2,1)S(1)}, u32[]{:S(2)}, u32[]{:S(2)}) %collective-permute-start.8) | collective-permute-done | bytes 360480 | tf_op jit(solution)/shard_map/ppermute | solution.py:27
  46.4 5.9 %collective-permute-start.9 = (bf16[64,2816]{1,0:T(8,128)(2,1)S(1)}, bf16[64,2816]{1,0:T(8,128)(2,1)S(1)}, u32[]{:S(2)}, u32[]{:S(2)}) collective-permute-start(bf16[64,2816]{1,0:T(8,128)(2,1)S(1)} %get-tuple-element.59), channel_id=1, source_target_pairs={{0,32},{32,0},{1,33},{33,1},{2,34},{34,2},{3,35},{35,3},{4,36},{36... | collective-permute-start | bytes 1081352 | tf_op jit(solution)/shard_map/ppermute | solution.py:27
  52.3 6.0 %collective-permute-done.18.b = bf16[64,2816]{1,0:T(8,128)(2,1)S(1)} collective-permute-done((bf16[64,2816]{1,0:T(8,128)(2,1)S(1)}, bf16[64,2816]{1,0:T(8,128)(2,1)S(1)}, u32[]{:S(2)}, u32[]{:S(2)}) %collective-permute-start.18) | collective-permute-done | bytes 360480 | tf_op jit(solution)/shard_map/ppermute | solution.py:27
  60.6 5.9 %collective-permute-start.20 = (bf16[64,2816]{1,0:T(8,128)(2,1)S(1)}, bf16[64,2816]{1,0:T(8,128)(2,1)S(1)}, u32[]{:S(2)}, u32[]{:S(2)}) collective-permute-start(bf16[64,2816]{1,0:T(8,128)(2,1)S(1)} %get-tuple-element.66), channel_id=1, source_target_pairs={{0,32},{32,0},{1,33},{33,1},{2,34},{34,2},{3,35},{35,3},{4,36},{36... | collective-permute-start | bytes 1081352 | tf_op jit(solution)/shard_map/ppermute | solution.py:27
  67.0 9.0 %collective-permute-start.10 = (bf16[64,2816]{1,0:T(8,128)(2,1)S(1)}, bf16[64,2816]{1,0:T(8,128)(2,1)S(1)}, u32[]{:S(2)}, u32[]{:S(2)}) collective-permute-start(bf16[64,2816]{1,0:T(8,128)(2,1)S(1)} %shard_map.104.a_0_), channel_id=1, source_target_pairs={{0,192},{64,0},{128,64},{192,128},{1,193},{65,1},{129,65},{193,129... | collective-permute-start | bytes 1081352 | tf_op jit(solution)/shard_map/ppermute | solution.py:27
  76.0 2.2 %collective-permute-start.12 = (bf16[64,2816]{1,0:T(8,128)(2,1)S(1)}, bf16[64,2816]{1,0:T(8,128)(2,1)S(1)}, u32[]{:S(2)}, u32[]{:S(2)}) collective-permute-start(bf16[64,2816]{1,0:T(8,128)(2,1)S(1)} %shard_map.104.a_0_), channel_id=1, source_target_pairs={{0,64},{64,128},{128,192},{192,0},{1,65},{65,129},{129,193},{193,1... | collective-permute-start | bytes 1081352 | tf_op jit(solution)/shard_map/ppermute | solution.py:27
  78.2 6.6 %collective-permute-done.20.other = bf16[64,2816]{1,0:T(8,128)(2,1)S(1)} collective-permute-done((bf16[64,2816]{1,0:T(8,128)(2,1)S(1)}, bf16[64,2816]{1,0:T(8,128)(2,1)S(1)}, u32[]{:S(2)}, u32[]{:S(2)}) %collective-permute-start.20) | collective-permute-done | bytes 360480 | tf_op jit(solution)/shard_map/ppermute | solution.py:27
  86.7 4.2 %collective-permute-start.22 = (bf16[64,1920]{1,0:T(8,128)(2,1)S(1)}, bf16[64,1920]{1,0:T(8,128)(2,1)S(1)}, u32[]{:S(2)}, u32[]{:S(2)}) collective-permute-start(bf16[64,1920]{1,0:T(8,128)(2,1)S(1)} %get-tuple-element.67.a_0_), channel_id=1, source_target_pairs={{0,128},{64,192},{128,0},{192,64},{1,129},{65,193},{129,1},{193,65... | collective-permute-start | bytes 737288 | tf_op jit(solution)/shard_map/ppermute | solution.py:27
  95.6 2.1 %collective-permute-done.22.a_2_ = bf16[64,1920]{1,0:T(8,128)(2,1)S(1)} collective-permute-done((bf16[64,1920]{1,0:T(8,128)(2,1)S(1)}, bf16[64,1920]{1,0:T(8,128)(2,1)S(1)}, u32[]{:S(2)}, u32[]{:S(2)}) %collective-permute-start.22) | collective-permute-done | bytes 245792 | tf_op jit(solution)/shard_map/ppermute | solution.py:27
  97.7 4.3 %collective-permute-done.23.a_3_ = bf16[64,1920]{1,0:T(8,128)(2,1)S(1)} collective-permute-done((bf16[64,1920]{1,0:T(8,128)(2,1)S(1)}, bf16[64,1920]{1,0:T(8,128)(2,1)S(1)}, u32[]{:S(2)}, u32[]{:S(2)}) %collective-permute-start.23) | collective-permute-done | bytes 245792 | tf_op jit(solution)/shard_map/ppermute | solution.py:27
  103.7 2.0 %collective-permute-done.25.refs_3_ = f32[136,1152]{1,0:T(8,128)S(1)} collective-permute-done((f32[136,1152]{1,0:T(8,128)S(1)}, f32[136,1152]{1,0:T(8,128)S(1)}, u32[]{:S(2)}, u32[]{:S(2)}) %collective-permute-start.25) | collective-permute-done | bytes 626720 | tf_op jit(solution)/shard_map/ppermute | solution.py:27
  108.3 2.9 %collective-permute-start.28 = (bf16[64,1280]{1,0:T(8,128)(2,1)S(1)}, bf16[64,1280]{1,0:T(8,128)(2,1)S(1)}, u32[]{:S(2)}, u32[]{:S(2)}) collective-permute-start(bf16[64,1280]{1,0:T(8,128)(2,1)S(1)} %get-tuple-element.81), channel_id=1, source_target_pairs={{0,16},{8,24},{16,0},{24,8},{1,17},{9,25},{17,1},{25,9},{2,18},{10... | collective-permute-start | bytes 491528 | tf_op jit(solution)/shard_map/ppermute | solution.py:27
  111.8 3.3 %collective-permute-start.33 = (bf16[64,896]{1,0:T(8,128)(2,1)S(1)}, bf16[64,896]{1,0:T(8,128)(2,1)S(1)}, u32[]{:S(2)}, u32[]{:S(2)}) collective-permute-start(bf16[64,896]{1,0:T(8,128)(2,1)S(1)} %get-tuple-element.94.a_0_), channel_id=1, source_target_pairs={{0,128},{64,192},{128,0},{192,64},{1,129},{65,193},{129,1},{193,65... | collective-permute-start | bytes 344072 | tf_op jit(solution)/shard_map/ppermute | solution.py:27
  116.8 2.1 %shard_map.113 = bf16[1024,896]{1,0:T(8,128)(2,1)} custom-call(bf16[64,1920]{1,0:T(8,128)(2,1)S(1)} %get-tuple-element.67.a_0_, bf16[64,1920]{1,0:T(8,128)(2,1)S(1)} %collective-permute-done.21.a_1_, bf16[64,1920]{1,0:T(8,128)(2,1)S(1)} %collective-permute-done.22.a_2_, bf16[64,1920]{1,0:T(8,128)(2,1)S(1)} %collective-permute-done.23.a_3_, ...), custom_call_target="tpu_custom_call" | custom-call | tf_op jit(solution)/shard_map/pallas_call | solution.py:48
  118.8 2.1 %shard_map.114 = bf16[1024,896]{1,0:T(8,128)(2,1)} custom-call(bf16[64,1920]{1,0:T(8,128)(2,1)S(1)} %get-tuple-element.67.a_0_, bf16[64,1920]{1,0:T(8,128)(2,1)S(1)} %collective-permute-done.21.a_1_, bf16[64,1920]{1,0:T(8,128)(2,1)S(1)} %collective-permute-done.22.a_2_, bf16[64,1920]{1,0:T(8,128)(2,1)S(1)} %collective-permute-done.23.a_3_, ...), custom_call_target="tpu_custom_call" | custom-call | tf_op jit(solution)/shard_map/pallas_call | solution.py:48
  121.2 3.8 %collective-permute-start.30 = (bf16[16,1408]{1,0:T(8,128)(2,1)S(1)}, bf16[16,1408]{1,0:T(8,128)(2,1)S(1)}, u32[]{:S(2)}, u32[]{:S(2)}) collective-permute-start(bf16[16,1408]{1,0:T(8,128)(2,1)S(1)} %get-tuple-element.87), channel_id=1, source_target_pairs={{0,4},{2,6},{4,0},{6,2},{1,5},{3,7},{5,1},{7,3},{8,12},{10,14},{12... | collective-permute-start | bytes 135176 | tf_op jit(solution)/shard_map/ppermute | solution.py:27
  125.1 1.9 %shard_map.116 = bf16[896,1024]{1,0:T(8,128)(2,1)} custom-call(bf16[64,896]{1,0:T(8,128)(2,1)S(1)} %get-tuple-element.94.a_0_, bf16[64,896]{1,0:T(8,128)(2,1)S(1)} %collective-permute-done.32.a_1_, bf16[64,896]{1,0:T(8,128)(2,1)S(1)} %collective-permute-done.33.a_2_, bf16[64,896]{1,0:T(8,128)(2,1)S(1)} %collective-permute-done.34.a_3_, ...), custom_call_target="tpu_custom_call" | custom-call | tf_op jit(solution)/shard_map/pallas_call | solution.py:48
  (69 shorter events, 40.4 us)
Async XLA Ops:
  11.6 9.0 %collective-permute-start.4 = (bf16[4,2,16,1024]{3,2,1,0:T(8,128)(2,1)S(1)}, bf16[4,2,16,1024]{3,2,1,0:T(8,128)(2,1)S(1)}, u32[]{:S(2)}, u32[]{:S(2)}) collective-permute-start(bf16[4,2,16,1024]{3,2,1,0:T(8,128)(2,1)S(1)} %pad_maximum_fusion.a_0_.a_4_), channel_id=1, source_target_pairs={{0,8},{8,16},{16,24},{24,0},{1,9},{9,17},{17,25},{25,1},{2,10},{10... | collective-permute-start | bytes 786440 | tf_op jit(solution)/shard_map/ppermute | solution.py:27
  20.6 9.1 %collective-permute-start.13 = (bf16[4,2,16,1024]{3,2,1,0:T(8,128)(2,1)S(1)}, bf16[4,2,16,1024]{3,2,1,0:T(8,128)(2,1)S(1)}, u32[]{:S(2)}, u32[]{:S(2)}) collective-permute-start(bf16[4,2,16,1024]{3,2,1,0:T(8,128)(2,1)S(1)} %pad_maximum_fusion.a_0_.a_4_), channel_id=1, source_target_pairs={{0,24},{8,0},{16,8},{24,16},{1,25},{9,1},{17,9},{25,17},{2,26},{10... | collective-permute-start | bytes 786440 | tf_op jit(solution)/shard_map/ppermute | solution.py:27
  22.3 9.9 %collective-permute-start.15 = (bf16[4,2,16,1024]{3,2,1,0:T(8,128)(2,1)S(1)}, bf16[4,2,16,1024]{3,2,1,0:T(8,128)(2,1)S(1)}, u32[]{:S(2)}, u32[]{:S(2)}) collective-permute-start(bf16[4,2,16,1024]{3,2,1,0:T(8,128)(2,1)S(1)} %pad_maximum_fusion.a_0_.a_4_), channel_id=1, source_target_pairs={{0,16},{8,24},{16,0},{24,8},{1,17},{9,25},{17,1},{25,9},{2,18},{10... | collective-permute-start | bytes 786440 | tf_op jit(solution)/shard_map/ppermute | solution.py:27
  24.8 13.1 %collective-permute-start.6 = (bf16[64,2816]{1,0:T(8,128)(2,1)S(1)}, bf16[64,2816]{1,0:T(8,128)(2,1)S(1)}, u32[]{:S(2)}, u32[]{:S(2)}) collective-permute-start(bf16[64,2816]{1,0:T(8,128)(2,1)S(1)} %get-tuple-element.55), channel_id=1, source_target_pairs={{0,64},{64,128},{128,192},{192,0},{1,65},{65,129},{129,193},{193,1... | collective-permute-start | bytes 1081352 | tf_op jit(solution)/shard_map/ppermute | solution.py:27
  26.1 17.8 %collective-permute-start.7 = (bf16[64,2816]{1,0:T(8,128)(2,1)S(1)}, bf16[64,2816]{1,0:T(8,128)(2,1)S(1)}, u32[]{:S(2)}, u32[]{:S(2)}) collective-permute-start(bf16[64,2816]{1,0:T(8,128)(2,1)S(1)} %get-tuple-element.56), channel_id=1, source_target_pairs={{0,128},{64,192},{128,0},{192,64},{1,129},{65,193},{129,1},{193,65... | collective-permute-start | bytes 1081352 | tf_op jit(solution)/shard_map/ppermute | solution.py:27
  26.9 19.1 %collective-permute-start.8 = (bf16[64,2816]{1,0:T(8,128)(2,1)S(1)}, bf16[64,2816]{1,0:T(8,128)(2,1)S(1)}, u32[]{:S(2)}, u32[]{:S(2)}) collective-permute-start(bf16[64,2816]{1,0:T(8,128)(2,1)S(1)} %get-tuple-element.57), channel_id=1, source_target_pairs={{0,192},{64,0},{128,64},{192,128},{1,193},{65,1},{129,65},{193,129... | collective-permute-start | bytes 1081352 | tf_op jit(solution)/shard_map/ppermute | solution.py:27
  35.7 16.7 %collective-permute-start.17 = (bf16[64,2816]{1,0:T(8,128)(2,1)S(1)}, bf16[64,2816]{1,0:T(8,128)(2,1)S(1)}, u32[]{:S(2)}, u32[]{:S(2)}) collective-permute-start(bf16[64,2816]{1,0:T(8,128)(2,1)S(1)} %get-tuple-element.62), channel_id=1, source_target_pairs={{0,64},{64,128},{128,192},{192,0},{1,65},{65,129},{129,193},{193,1... | collective-permute-start | bytes 1081352 | tf_op jit(solution)/shard_map/ppermute | solution.py:27
  37.1 21.2 %collective-permute-start.18 = (bf16[64,2816]{1,0:T(8,128)(2,1)S(1)}, bf16[64,2816]{1,0:T(8,128)(2,1)S(1)}, u32[]{:S(2)}, u32[]{:S(2)}) collective-permute-start(bf16[64,2816]{1,0:T(8,128)(2,1)S(1)} %get-tuple-element.63), channel_id=1, source_target_pairs={{0,128},{64,192},{128,0},{192,64},{1,129},{65,193},{129,1},{193,65... | collective-permute-start | bytes 1081352 | tf_op jit(solution)/shard_map/ppermute | solution.py:27
  37.9 22.3 %collective-permute-start.19 = (bf16[64,2816]{1,0:T(8,128)(2,1)S(1)}, bf16[64,2816]{1,0:T(8,128)(2,1)S(1)}, u32[]{:S(2)}, u32[]{:S(2)}) collective-permute-start(bf16[64,2816]{1,0:T(8,128)(2,1)S(1)} %get-tuple-element.64), channel_id=1, source_target_pairs={{0,192},{64,0},{128,64},{192,128},{1,193},{65,1},{129,65},{193,129... | collective-permute-start | bytes 1081352 | tf_op jit(solution)/shard_map/ppermute | solution.py:27
  46.4 20.1 %collective-permute-start.9 = (bf16[64,2816]{1,0:T(8,128)(2,1)S(1)}, bf16[64,2816]{1,0:T(8,128)(2,1)S(1)}, u32[]{:S(2)}, u32[]{:S(2)}) collective-permute-start(bf16[64,2816]{1,0:T(8,128)(2,1)S(1)} %get-tuple-element.59), channel_id=1, source_target_pairs={{0,32},{32,0},{1,33},{33,1},{2,34},{34,2},{3,35},{35,3},{4,36},{36... | collective-permute-start | bytes 1081352 | tf_op jit(solution)/shard_map/ppermute | solution.py:27
  60.6 24.1 %collective-permute-start.20 = (bf16[64,2816]{1,0:T(8,128)(2,1)S(1)}, bf16[64,2816]{1,0:T(8,128)(2,1)S(1)}, u32[]{:S(2)}, u32[]{:S(2)}) collective-permute-start(bf16[64,2816]{1,0:T(8,128)(2,1)S(1)} %get-tuple-element.66), channel_id=1, source_target_pairs={{0,32},{32,0},{1,33},{33,1},{2,34},{34,2},{3,35},{35,3},{4,36},{36... | collective-permute-start | bytes 1081352 | tf_op jit(solution)/shard_map/ppermute | solution.py:27
  67.0 23.9 %collective-permute-start.10 = (bf16[64,2816]{1,0:T(8,128)(2,1)S(1)}, bf16[64,2816]{1,0:T(8,128)(2,1)S(1)}, u32[]{:S(2)}, u32[]{:S(2)}) collective-permute-start(bf16[64,2816]{1,0:T(8,128)(2,1)S(1)} %shard_map.104.a_0_), channel_id=1, source_target_pairs={{0,192},{64,0},{128,64},{192,128},{1,193},{65,1},{129,65},{193,129... | collective-permute-start | bytes 1081352 | tf_op jit(solution)/shard_map/ppermute | solution.py:27
  76.0 14.9 %collective-permute-start.11 = (bf16[64,2816]{1,0:T(8,128)(2,1)S(1)}, bf16[64,2816]{1,0:T(8,128)(2,1)S(1)}, u32[]{:S(2)}, u32[]{:S(2)}) collective-permute-start(bf16[64,2816]{1,0:T(8,128)(2,1)S(1)} %shard_map.104.a_0_), channel_id=1, source_target_pairs={{0,128},{64,192},{128,0},{192,64},{1,129},{65,193},{129,1},{193,65... | collective-permute-start | bytes 1081352 | tf_op jit(solution)/shard_map/ppermute | solution.py:27
  76.0 14.9 %collective-permute-start.12 = (bf16[64,2816]{1,0:T(8,128)(2,1)S(1)}, bf16[64,2816]{1,0:T(8,128)(2,1)S(1)}, u32[]{:S(2)}, u32[]{:S(2)}) collective-permute-start(bf16[64,2816]{1,0:T(8,128)(2,1)S(1)} %shard_map.104.a_0_), channel_id=1, source_target_pairs={{0,64},{64,128},{128,192},{192,0},{1,65},{65,129},{129,193},{193,1... | collective-permute-start | bytes 1081352 | tf_op jit(solution)/shard_map/ppermute | solution.py:27
  85.2 10.4 %collective-permute-start.21 = (bf16[64,1920]{1,0:T(8,128)(2,1)S(1)}, bf16[64,1920]{1,0:T(8,128)(2,1)S(1)}, u32[]{:S(2)}, u32[]{:S(2)}) collective-permute-start(bf16[64,1920]{1,0:T(8,128)(2,1)S(1)} %get-tuple-element.67.a_0_), channel_id=1, source_target_pairs={{0,192},{64,0},{128,64},{192,128},{1,193},{65,1},{129,65},{193,129... | collective-permute-start | bytes 737288 | tf_op jit(solution)/shard_map/ppermute | solution.py:27
  86.7 11.0 %collective-permute-start.22 = (bf16[64,1920]{1,0:T(8,128)(2,1)S(1)}, bf16[64,1920]{1,0:T(8,128)(2,1)S(1)}, u32[]{:S(2)}, u32[]{:S(2)}) collective-permute-start(bf16[64,1920]{1,0:T(8,128)(2,1)S(1)} %get-tuple-element.67.a_0_), channel_id=1, source_target_pairs={{0,128},{64,192},{128,0},{192,64},{1,129},{65,193},{129,1},{193,65... | collective-permute-start | bytes 737288 | tf_op jit(solution)/shard_map/ppermute | solution.py:27
  90.9 11.1 %collective-permute-start.23 = (bf16[64,1920]{1,0:T(8,128)(2,1)S(1)}, bf16[64,1920]{1,0:T(8,128)(2,1)S(1)}, u32[]{:S(2)}, u32[]{:S(2)}) collective-permute-start(bf16[64,1920]{1,0:T(8,128)(2,1)S(1)} %get-tuple-element.67.a_0_), channel_id=1, source_target_pairs={{0,64},{64,128},{128,192},{192,0},{1,65},{65,129},{129,193},{193,1... | collective-permute-start | bytes 737288 | tf_op jit(solution)/shard_map/ppermute | solution.py:27
  94.1 9.6 %collective-permute-start.24 = (f32[136,1152]{1,0:T(8,128)S(1)}, f32[136,1152]{1,0:T(8,128)S(1)}, u32[]{:S(2)}, u32[]{:S(2)}) collective-permute-start(f32[136,1152]{1,0:T(8,128)S(1)} %get-tuple-element.75), channel_id=1, source_target_pairs={{0,1},{1,0},{2,3},{3,2},{4,5},{5,4},{6,7},{7,6},{8,9},{9,8},{10,11... | collective-permute-start | bytes 1880072 | tf_op jit(solution)/shard_map/ppermute | solution.py:27
  106.2 8.9 %collective-permute-start.26 = (bf16[64,1280]{1,0:T(8,128)(2,1)S(1)}, bf16[64,1280]{1,0:T(8,128)(2,1)S(1)}, u32[]{:S(2)}, u32[]{:S(2)}) collective-permute-start(bf16[64,1280]{1,0:T(8,128)(2,1)S(1)} %get-tuple-element.79), channel_id=1, source_target_pairs={{0,24},{8,0},{16,8},{24,16},{1,25},{9,1},{17,9},{25,17},{2,26},{10... | collective-permute-start | bytes 491528 | tf_op jit(solution)/shard_map/ppermute | solution.py:27
  106.7 14.2 %collective-permute-start.27 = (bf16[64,1280]{1,0:T(8,128)(2,1)S(1)}, bf16[64,1280]{1,0:T(8,128)(2,1)S(1)}, u32[]{:S(2)}, u32[]{:S(2)}) collective-permute-start(bf16[64,1280]{1,0:T(8,128)(2,1)S(1)} %get-tuple-element.80), channel_id=1, source_target_pairs={{0,8},{8,16},{16,24},{24,0},{1,9},{9,17},{17,25},{25,1},{2,10},{10... | collective-permute-start | bytes 491528 | tf_op jit(solution)/shard_map/ppermute | solution.py:27
  108.3 12.6 %collective-permute-start.28 = (bf16[64,1280]{1,0:T(8,128)(2,1)S(1)}, bf16[64,1280]{1,0:T(8,128)(2,1)S(1)}, u32[]{:S(2)}, u32[]{:S(2)}) collective-permute-start(bf16[64,1280]{1,0:T(8,128)(2,1)S(1)} %get-tuple-element.81), channel_id=1, source_target_pairs={{0,16},{8,24},{16,0},{24,8},{1,17},{9,25},{17,1},{25,9},{2,18},{10... | collective-permute-start | bytes 491528 | tf_op jit(solution)/shard_map/ppermute | solution.py:27
  111.2 13.8 %collective-permute-start.32 = (bf16[64,896]{1,0:T(8,128)(2,1)S(1)}, bf16[64,896]{1,0:T(8,128)(2,1)S(1)}, u32[]{:S(2)}, u32[]{:S(2)}) collective-permute-start(bf16[64,896]{1,0:T(8,128)(2,1)S(1)} %get-tuple-element.94.a_0_), channel_id=1, source_target_pairs={{0,192},{64,0},{128,64},{192,128},{1,193},{65,1},{129,65},{193,129... | collective-permute-start | bytes 344072 | tf_op jit(solution)/shard_map/ppermute | solution.py:27
  111.8 13.3 %collective-permute-start.33 = (bf16[64,896]{1,0:T(8,128)(2,1)S(1)}, bf16[64,896]{1,0:T(8,128)(2,1)S(1)}, u32[]{:S(2)}, u32[]{:S(2)}) collective-permute-start(bf16[64,896]{1,0:T(8,128)(2,1)S(1)} %get-tuple-element.94.a_0_), channel_id=1, source_target_pairs={{0,128},{64,192},{128,0},{192,64},{1,129},{65,193},{129,1},{193,65... | collective-permute-start | bytes 344072 | tf_op jit(solution)/shard_map/ppermute | solution.py:27
  115.0 10.0 %collective-permute-start.34 = (bf16[64,896]{1,0:T(8,128)(2,1)S(1)}, bf16[64,896]{1,0:T(8,128)(2,1)S(1)}, u32[]{:S(2)}, u32[]{:S(2)}) collective-permute-start(bf16[64,896]{1,0:T(8,128)(2,1)S(1)} %get-tuple-element.94.a_0_), channel_id=1, source_target_pairs={{0,64},{64,128},{128,192},{192,0},{1,65},{65,129},{129,193},{193,1... | collective-permute-start | bytes 344072 | tf_op jit(solution)/shard_map/ppermute | solution.py:27
  (13 other events, 68.4 us)

commit v3 on v2

--- a/solution.py
+++ b/solution.py
@@ -7,6 +7,7 @@
 from jax.sharding import PartitionSpec as P
 
 D = 8192
+FF = 28672
 BF = jnp.bfloat16
 F32 = jnp.float32
 LANES = 128
@@ -16,6 +17,8 @@
 STEPS = (0, 1, -1, 2)
 PARTS = 4
 GROUPS = ((0, 1), (2, 3))
+END = 16
+WIDTH = FF // 32
 GAINS = GROUPS[-1]
 
 
@@ -38,6 +41,35 @@
             rest = rest - piece
             at += 1
     return out
+
+
+def spots(rows):
+    line = lax.broadcasted_iota(jnp.int32, (rows, LANES), 0)
+    return line == lax.broadcasted_iota(jnp.int32, (rows, LANES), 1)
+
+
+def lay(*columns):
+    line = lax.broadcasted_iota(jnp.int32, (END, LANES), 0)
+    out, at = jnp.zeros((END, LANES), F32), 0
+    for column in columns:
+        rest = jnp.sum(jnp.where(spots(column.shape[0]), column, 0.0), axis=0, keepdims=True)
+        for _ in range(3):
+            piece = rest.astype(BF).astype(F32)
+            out = jnp.where(line == at, piece, out)
+            rest = rest - piece
+            at += 1
+    return out
+
+
+def stand(block, at, rows):
+    row = block[at : at + 1] + block[at + 1 : at + 2] + block[at + 2 : at + 3]
+    return jnp.sum(jnp.where(spots(rows), row, 0.0), axis=1, keepdims=True)
+
+
+def tiles(ref, start, width, rows):
+    return jnp.concatenate(
+        [ref[start + j * rows : start + j * rows + rows] for j in range(width // LANES)], axis=1
+    )
 
 
 def head(block, at):
@@ -124,45 +156,55 @@
     grad = tokens(blocks, 1)
     rows, width = 32 * size, gate_w.shape[1]
 
+    cuts = width // LANES
+
     def put(value, start):
         for s in range(4):
-            part = value[rows * s : rows * s + rows]
-            outs[s][:, start : start + value.shape[1]] = part.astype(outs[s].dtype)
+            for j in range(cuts):
+                part = value[rows * s : rows * s + rows, j * LANES : j * LANES + LANES]
+                at = (start + j) * rows
+                outs[s][at : at + rows] = part.astype(outs[s].dtype)
 
     put(jnp.dot(scaled, gate_w[...], preferred_element_type=F32), 0)
-    put(jnp.dot(scaled, up_w[...], preferred_element_type=F32), width)
+    put(jnp.dot(scaled, up_w[...], preferred_element_type=F32), cuts)
     put(
         lax.dot_general(grad, down_w[...], CONTRACT_LAST, preferred_element_type=F32),
-        2 * width,
-    )
-    put(tail(jnp.sum(x * x, axis=1, keepdims=True)), 3 * width)
+        2 * cuts,
+    )
+    square = jnp.sum(x * x, axis=1, keepdims=True)
+    for s in range(4):
+        outs[s][3 * cuts * rows :] = lay(square[rows * s : rows * s + rows]).astype(outs[s].dtype)
 
 
 def add_x(own, a, b, c, total, out):
     value = own[...] + a[...].astype(F32) + b[...].astype(F32) + c[...].astype(F32)
-    end = tail(head(value[:, -LANES:], 0))
-    value = jnp.concatenate([value[:, :-LANES], end], axis=1)
-    total[...] = value
-    out[...] = value.astype(BF)
+    end = lay(stand(value[-END:], 0, LANES))
+    total[:-END], total[-END:] = value[:-END], end
+    out[:-END], out[-END:] = value[:-END].astype(BF), end.astype(BF)
 
 
 def activate(own, other, out, hidden=None):
     total = own[...] + other[...].astype(F32)
-    width = (total.shape[1] - LANES) // 3
-    inv = lax.rsqrt(head(total[:, -LANES:], 0) / D + 1e-05)
-    gate = total[:, :width] * inv
-    up = total[:, width : 2 * width] * inv
-    back = total[:, 2 * width : 3 * width]
+    size = (total.shape[0] - END) // 3
+    rows = size * LANES // WIDTH
+    inv = lax.rsqrt(stand(total[-END:], 0, rows) / D + 1e-05)
+    every = jnp.concatenate([inv] * (size // rows), axis=0)
+    gate = total[:size] * every
+    up = total[size : 2 * size] * every
+    back = total[2 * size : 3 * size]
     sig = 1.0 / (1.0 + jnp.exp(-gate))
     silu = gate * sig
     d_gate = back * up * sig * (1.0 + gate * (1.0 - sig))
     d_up = back * silu
-    mean = jnp.sum(d_gate * gate + d_up * up, axis=1, keepdims=True)
-    out[:, :width] = d_gate.astype(BF)
-    out[:, width : 2 * width] = d_up.astype(BF)
-    out[:, 2 * width : 2 * width + LANES] = tail(inv, mean).astype(BF)
+    terms = d_gate * gate + d_up * up
+    mean = jnp.sum(
+        sum(terms[at : at + rows] for at in range(0, size, rows)), axis=1, keepdims=True
+    )
+    out[:size] = d_gate.astype(BF)
+    out[size : 2 * size] = d_up.astype(BF)
+    out[2 * size : 2 * size + END] = lay(inv, mean).astype(BF)
     if hidden is None:
-        out[:, 2 * width + LANES :] = (silu * up).astype(BF)
+        out[2 * size + END :] = (silu * up).astype(BF)
     else:
         hidden[...] = (silu * up).astype(BF)
 
@@ -172,17 +214,17 @@
     gate_w, up_w, last_gain, mine, theirs, inv_out, gain_out = refs[4 + 2 * size :]
     rows, (depth, width) = 32 * size, gate_w.shape
 
-    def rows_of(start, stop):
-        return jnp.concatenate([m[:, start:stop] for m in messages], axis=0)
+    size_of = rows * width // LANES
+
+    def rows_of(at):
+        return jnp.concatenate([tiles(m, at * size_of, width, rows) for m in messages], axis=0)
 
     part = lax.dot_general(
-        rows_of(0, width), gate_w[...], CONTRACT_LAST, preferred_element_type=F32
-    ) + lax.dot_general(
-        rows_of(width, 2 * width), up_w[...], CONTRACT_LAST, preferred_element_type=F32
-    )
-    end = rows_of(2 * width, 2 * width + LANES).astype(F32)
-    inv = head(end, 0)
-    mean = tail(head(end, 3))
+        rows_of(0), gate_w[...], CONTRACT_LAST, preferred_element_type=F32
+    ) + lax.dot_general(rows_of(1), up_w[...], CONTRACT_LAST, preferred_element_type=F32)
+    ends = [m[2 * size_of : 2 * size_of + END].astype(F32) for m in messages]
+    inv = jnp.concatenate([stand(e, 0, rows) for e in ends], axis=0)
+    mean = tail(jnp.concatenate([stand(e, 3, rows) for e in ends], axis=0))
     x = tokens(blocks, 0).astype(F32)
     gain = last_gain[...] + jnp.sum(part * x * inv, axis=0, keepdims=True)
     for s in range(4):
@@ -192,11 +234,12 @@
             place = pl.ds(pl.multiple_of(64 * i + 16 * at, 16), 16)
             for core, out in enumerate((mine, theirs)):
                 start = rows * s + 32 * i + 16 * core
-                out[place, :depth] = part[start : start + 16]
-                out[place, depth:] = mean[start : start + 16]
+                out[place, :depth] = part[start : start + 16].astype(out.dtype)
+                out[place, depth:] = mean[start : start + 16].astype(out.dtype)
     gain_out[...] = gain
-    theirs[64 * size :, :depth] = jnp.broadcast_to(gain, (8, depth))
-    theirs[64 * size :, depth:] = jnp.zeros((8, LANES), F32)
+    packed = pack(gain, END)
+    theirs[64 * size :, : packed.shape[1]] = packed
+    theirs[64 * size :, packed.shape[1] :] = jnp.zeros((END, depth + LANES - packed.shape[1]), BF)
 
 
 def add_core(*refs):
@@ -204,11 +247,11 @@
     mine, received, gains, outs = refs[:count], refs[count : 2 * count], refs[-5], refs[-4:]
     depth = gains.shape[1]
     last = 64 * len(GROUPS[-1])
-    packed = pack(gains[...] + received[-1][last : last + 1, :depth], 64)
+    packed = pack(gains[...] + unpack(received[-1][last : last + END, : 2 * LANES], depth), 64)
     for g, group in enumerate(GROUPS):
         for i, block in enumerate(group):
             rows = slice(64 * i, 64 * i + 64)
-            value, out = mine[g][rows] + received[g][rows], outs[block]
+            value, out = mine[g][rows] + received[g][rows].astype(F32), outs[block]
             out[:, :depth] = value[:, :depth].astype(BF)
             out[:, depth : depth + LANES] = tail(head(value[:, depth:], 0)).astype(BF)
             out[:, depth + LANES :] = packed
@@ -252,31 +295,32 @@
     return lax.dot_general(left, right, CONTRACT_FIRST, preferred_element_type=F32)
 
 
-def columns(messages, start, stop):
-    return jnp.concatenate([m[:, start:stop] for m in messages], axis=0)
+def columns(messages, start, width, rows):
+    return jnp.concatenate([tiles(m, start, width, rows) for m in messages], axis=0)
 
 
 def early_grads(group, *refs):
     refs, outs = refs[:-3], refs[-3:]
     normed, grad = operands(group, refs)
-    width = outs[0].shape[1]
-    top = refs[0].shape[1]
+    width, rows = outs[0].shape[1], 32 * len(group)
+    size = rows * width // LANES
     for at in (0, 1):
-        outs[at][...] = product(normed, columns(refs[:4], at * width, at * width + width))
-    outs[2][...] = product(columns(refs[:4], top - width, top), grad)
+        outs[at][...] = product(normed, columns(refs[:4], at * size, width, rows))
+    outs[2][...] = product(columns(refs[:4], 2 * size + END, width, rows), grad)
 
 
 def wide_grads(at, group, *refs):
     refs, total, out = refs[:-2], refs[-2], refs[-1]
     normed, _ = operands(group, refs)
-    width = out.shape[1]
-    part = product(normed, columns(refs[:4], at * width, at * width + width))
+    width, rows = out.shape[1], 32 * len(group)
+    start = at * rows * width // LANES
+    part = product(normed, columns(refs[:4], start, width, rows))
     out[...] = (total[...] + part).astype(BF)
 
 
 def down_grads(group, *refs):
     hidden, blocks, total, out = refs[:4], pairs(refs[4:-2]), refs[-2], refs[-1]
-    part = product(jnp.concatenate([h[...] for h in hidden], axis=0), tokens(blocks, 1))
+    part = product(columns(hidden, 0, out.shape[0], 32 * len(group)), tokens(blocks, 1))
     out[...] = (total[...] + part).astype(BF)
 
 
@@ -287,7 +331,7 @@
 def shards(activations, out_grad, norm_gain, gate_w, up_w, down_w):
     rows, depth = activations.shape
     width = gate_w.shape[1]
-    wide, deep = 3 * width + LANES, depth + LANES
+    deep = depth + LANES
     gain = norm_gain[None, :]
 
     gate_w, up_w, down_w = load([gate_w, up_w, down_w])
@@ -302,15 +346,15 @@
 
     totals, crossed = [], []
     for group in GROUPS:
-        tall = 32 * len(group)
+        size = 32 * len(group) * width // LANES
         s0, s1, s2, s3 = call(
             lambda *a, n=len(group): forward(n, *a),
-            [((tall, wide), F32)] + [((tall, wide), BF)] * 3,
+            [((3 * size + END, LANES), F32)] + [((3 * size + END, LANES), BF)] * 3,
             [*members(group), gain, gate_w, up_w, down_w],
         )
         total, out = call(
             add_x,
-            [((tall, wide), F32), ((tall, wide), BF)],
+            [((3 * size + END, LANES), F32), ((3 * size + END, LANES), BF)],
             [s0, send(s1, "x", 1), send(s2, "x", 2), send(s3, "x", -1)],
         )
         totals.append(total)
@@ -321,15 +365,16 @@
     for group, total, arrived in zip(GROUPS, totals, crossed):
         size = len(group)
         tall = 32 * size
+        cut = tall * width // LANES
         if len(invs) < len(GROUPS) - 1:
-            shapes = [((tall, wide), BF)]
+            shapes = [((3 * cut + END, LANES), BF)]
         else:
-            shapes = [((tall, 2 * width + LANES), BF), ((tall, width), BF)]
+            shapes = [((2 * cut + END, LANES), BF), ((cut, LANES), BF)]
         m0, *hidden = call(activate, shapes, [total, arrived])
         found = [m0, send(m0, "x", -1), send(m0, "x", 2), send(m0, "x", 1)]
         mine, theirs, inv, gains = call(
             lambda *a, n=size: backward(n, *a),
-            [((64 * size, deep), F32), ((64 * size + 8, deep), F32), ((4, tall, 1), F32)]
+            [((64 * size, deep), F32), ((64 * size + END, deep), BF), ((4, tall, 1), F32)]
             + [((1, depth), F32)],
             [*found, *members(group), gate_w, up_w, gains],
         )

time: 130 us -> 128 us (0.985)
  waiting for transfers between devices: 47.6 us -> 44.8 us
    ppermute x35, waiting for transfers between devices: 47.6 us -> 44.8 us  [send(): lax.ppermute(value, axis, ring(2 if axis in ('zh', 'core') else 4, step))]
  transfers between devices with their start and end apart: 35 -> 35, of which waited for: 19 -> 18; matrix products, arithmetic and copies ran while one was open for 0% -> 0% of each run, Pallas kernels for 14% -> 15%
where the time goes in v3:
time: 128 us; the launch traced here: 127 us
  starting transfers between devices  60.8 us (48%)
  waiting for transfers between devices  44.8 us (35%)
  Pallas kernels  20.1 us (16%)
    ppermute x35, starting transfers between devices, send(): lax.ppermute(value, axis, ring(2 if axis in ('zh', 'core') else 4, step))  60.8 us
    ppermute x35, waiting for transfers between devices, send(): lax.ppermute(value, axis, ring(2 if axis in ('zh', 'core') else 4, step))  44.8 us
    pallas_call x15, Pallas kernels, call(): pl.pallas_call(kernel, out_shape=[jax.ShapeDtypeStruct(s, d) for s, d in...  17.5 us
    pallas_call x1, Pallas kernels, load(): pl.pallas_call(kernel, out_shape=[jax.ShapeDtypeStruct(w.shape, w.dtype)...  2.64 us
  transfers between devices with their start and end apart: 35, of which 18 were waited for; matrix products, arithmetic and copies ran while one was open for 0% of the time, Pallas kernels for 15%

profile of v3, /device:TPU:4, one launch (start us, length us, event | category | flops | bytes accessed | tf_op | source)
XLA Modules:
  0.0 127.4 jit_solution(3935342461499963708)
XLA Ops:
  1.4 2.0 %collective-permute-start.2 = (bf16[2,16,1024]{2,1,0:T(8,128)(2,1)S(1)}, bf16[2,16,1024]{2,1,0:T(8,128)(2,1)S(1)}, u32[]{:S(2)}, u32[]{:S(2)}) collective-permute-start(bf16[2,16,1024]{2,1,0:T(8,128)(2,1)S(1)} %get-tuple-element.96), channel_id=1, source_target_pairs={{0,2},{2,4},{4,6},{6,0},{1,3},{3,5},{5,7},{7,1},{8,10},{10,12},{12... | collective-permute-start | bytes 196616 | tf_op jit(solution)/shard_map/ppermute | solution.py:30
  3.4 3.3 %collective-permute-start.1 = (bf16[2,16,1024]{2,1,0:T(8,128)(2,1)S(1)}, bf16[2,16,1024]{2,1,0:T(8,128)(2,1)S(1)}, u32[]{:S(2)}, u32[]{:S(2)}) collective-permute-start(bf16[2,16,1024]{2,1,0:T(8,128)(2,1)S(1)} %get-tuple-element.96), channel_id=1, source_target_pairs={{0,4},{2,6},{4,0},{6,2},{1,5},{3,7},{5,1},{7,3},{8,12},{10,14},{12... | collective-permute-start | bytes 196616 | tf_op jit(solution)/shard_map/ppermute | solution.py:30
  8.9 2.3 %collective-permute-done.1 = bf16[2,16,1024]{2,1,0:T(8,128)(2,1)S(1)} collective-permute-done((bf16[2,16,1024]{2,1,0:T(8,128)(2,1)S(1)}, bf16[2,16,1024]{2,1,0:T(8,128)(2,1)S(1)}, u32[]{:S(2)}, u32[]{:S(2)}) %collective-permute-start.1) | collective-permute-done | bytes 65568 | tf_op jit(solution)/shard_map/ppermute | solution.py:30
  13.2 2.6 %shard_map.101 = (bf16[1024,896]{1,0:T(8,128)(2,1)S(1)}, bf16[1024,896]{1,0:T(8,128)(2,1)S(1)}, bf16[896,1024]{1,0:T(8,128)(2,1)S(1)}) custom-call(bf16[1024,896]{1,0:T(8,128)(2,1)} %refs_0_.1, bf16[1024,896]{1,0:T(8,128)(2,1)} %refs_1_.1, bf16[896,1024]{1,0:T(8,128)(2,1)} %refs_2_.1), custom_call_target="tpu_custom_call" | custom-call | tf_op jit(solution)/shard_map/pallas_call | solution.py:104
  16.0 4.6 %collective-permute-done.4.a_2_.a_6_ = bf16[4,2,16,1024]{3,2,1,0:T(8,128)(2,1)S(1)} collective-permute-done((bf16[4,2,16,1024]{3,2,1,0:T(8,128)(2,1)S(1)}, bf16[4,2,16,1024]{3,2,1,0:T(8,128)(2,1)S(1)}, u32[]{:S(2)}, u32[]{:S(2)}) %collective-permute-start.4) | collective-permute-done | bytes 262176 | tf_op jit(solution)/shard_map/ppermute | solution.py:30
  29.7 2.6 %collective-permute-done.15.a_2_.a_6_ = bf16[4,2,16,1024]{3,2,1,0:T(8,128)(2,1)S(1)} collective-permute-done((bf16[4,2,16,1024]{3,2,1,0:T(8,128)(2,1)S(1)}, bf16[4,2,16,1024]{3,2,1,0:T(8,128)(2,1)S(1)}, u32[]{:S(2)}, u32[]{:S(2)}) %collective-permute-start.15) | collective-permute-done | bytes 262176 | tf_op jit(solution)/shard_map/ppermute | solution.py:30
  39.1 4.3 %collective-permute-done.7.b = bf16[1360,128]{1,0:T(8,128)(2,1)S(1)} collective-permute-done((bf16[1360,128]{1,0:T(8,128)(2,1)S(1)}, bf16[1360,128]{1,0:T(8,128)(2,1)S(1)}, u32[]{:S(2)}, u32[]{:S(2)}) %collective-permute-start.7) | collective-permute-done | bytes 348192 | tf_op jit(solution)/shard_map/ppermute | solution.py:30
  43.4 2.1 %collective-permute-done.8.c = bf16[1360,128]{1,0:T(8,128)(2,1)S(1)} collective-permute-done((bf16[1360,128]{1,0:T(8,128)(2,1)S(1)}, bf16[1360,128]{1,0:T(8,128)(2,1)S(1)}, u32[]{:S(2)}, u32[]{:S(2)}) %collective-permute-start.8) | collective-permute-done | bytes 348192 | tf_op jit(solution)/shard_map/ppermute | solution.py:30
  45.8 5.9 %collective-permute-start.9 = (bf16[1360,128]{1,0:T(8,128)(2,1)S(1)}, bf16[1360,128]{1,0:T(8,128)(2,1)S(1)}, u32[]{:S(2)}, u32[]{:S(2)}) collective-permute-start(bf16[1360,128]{1,0:T(8,128)(2,1)S(1)} %get-tuple-element.59), channel_id=1, source_target_pairs={{0,32},{32,0},{1,33},{33,1},{2,34},{34,2},{3,35},{35,3},{4,36},{36... | collective-permute-start | bytes 1044488 | tf_op jit(solution)/shard_map/ppermute | solution.py:30
  51.8 5.5 %collective-permute-done.18.b = bf16[1360,128]{1,0:T(8,128)(2,1)S(1)} collective-permute-done((bf16[1360,128]{1,0:T(8,128)(2,1)S(1)}, bf16[1360,128]{1,0:T(8,128)(2,1)S(1)}, u32[]{:S(2)}, u32[]{:S(2)}) %collective-permute-start.18) | collective-permute-done | bytes 348192 | tf_op jit(solution)/shard_map/ppermute | solution.py:30
  59.5 5.9 %collective-permute-start.20 = (bf16[1360,128]{1,0:T(8,128)(2,1)S(1)}, bf16[1360,128]{1,0:T(8,128)(2,1)S(1)}, u32[]{:S(2)}, u32[]{:S(2)}) collective-permute-start(bf16[1360,128]{1,0:T(8,128)(2,1)S(1)} %get-tuple-element.66), channel_id=1, source_target_pairs={{0,32},{32,0},{1,33},{33,1},{2,34},{34,2},{3,35},{35,3},{4,36},{36... | collective-permute-start | bytes 1044488 | tf_op jit(solution)/shard_map/ppermute | solution.py:30
  65.9 9.1 %collective-permute-start.10 = (bf16[1360,128]{1,0:T(8,128)(2,1)S(1)}, bf16[1360,128]{1,0:T(8,128)(2,1)S(1)}, u32[]{:S(2)}, u32[]{:S(2)}) collective-permute-start(bf16[1360,128]{1,0:T(8,128)(2,1)S(1)} %shard_map.104.a_0_), channel_id=1, source_target_pairs={{0,192},{64,0},{128,64},{192,128},{1,193},{65,1},{129,65},{193,129... | collective-permute-start | bytes 1044488 | tf_op jit(solution)/shard_map/ppermute | solution.py:30
  75.0 2.2 %collective-permute-start.12 = (bf16[1360,128]{1,0:T(8,128)(2,1)S(1)}, bf16[1360,128]{1,0:T(8,128)(2,1)S(1)}, u32[]{:S(2)}, u32[]{:S(2)}) collective-permute-start(bf16[1360,128]{1,0:T(8,128)(2,1)S(1)} %shard_map.104.a_0_), channel_id=1, source_target_pairs={{0,64},{64,128},{128,192},{192,0},{1,65},{65,129},{129,193},{193,1... | collective-permute-start | bytes 1044488 | tf_op jit(solution)/shard_map/ppermute | solution.py:30
  77.2 6.3 %collective-permute-done.20.other = bf16[1360,128]{1,0:T(8,128)(2,1)S(1)} collective-permute-done((bf16[1360,128]{1,0:T(8,128)(2,1)S(1)}, bf16[1360,128]{1,0:T(8,128)(2,1)S(1)}, u32[]{:S(2)}, u32[]{:S(2)}) %collective-permute-start.20) | collective-permute-done | bytes 348192 | tf_op jit(solution)/shard_map/ppermute | solution.py:30
  85.1 4.1 %collective-permute-start.22 = (bf16[912,128]{1,0:T(8,128)(2,1)S(1)}, bf16[912,128]{1,0:T(8,128)(2,1)S(1)}, u32[]{:S(2)}, u32[]{:S(2)}) collective-permute-start(bf16[912,128]{1,0:T(8,128)(2,1)S(1)} %get-tuple-element.67.a_0_), channel_id=1, source_target_pairs={{0,128},{64,192},{128,0},{192,64},{1,129},{65,193},{129,1},{193,65... | collective-permute-start | bytes 700424 | tf_op jit(solution)/shard_map/ppermute | solution.py:30
  90.7 1.9 %shard_map.109 = (f32[1024,896]{1,0:T(8,128)S(1)}, f32[1024,896]{1,0:T(8,128)S(1)}, f32[896,1024]{1,0:T(8,128)S(1)}) custom-call(bf16[1360,128]{1,0:T(8,128)(2,1)S(1)} %shard_map.104.a_0_, bf16[1360,128]{1,0:T(8,128)(2,1)S(1)} %collective-permute-done.10.a_1_, bf16[1360,128]{1,0:T(8,128)(2,1)S(1)} %collective-permute-done.11.a_2_, ...), custom_call_target="tpu_custom_call" | custom-call | tf_op jit(solution)/shard_map/pallas_call | solution.py:80
  93.7 2.1 %collective-permute-done.22.a_2_ = bf16[912,128]{1,0:T(8,128)(2,1)S(1)} collective-permute-done((bf16[912,128]{1,0:T(8,128)(2,1)S(1)}, bf16[912,128]{1,0:T(8,128)(2,1)S(1)}, u32[]{:S(2)}, u32[]{:S(2)}) %collective-permute-start.22) | collective-permute-done | bytes 233504 | tf_op jit(solution)/shard_map/ppermute | solution.py:30
  95.8 3.6 %collective-permute-done.23.a_3_ = bf16[912,128]{1,0:T(8,128)(2,1)S(1)} collective-permute-done((bf16[912,128]{1,0:T(8,128)(2,1)S(1)}, bf16[912,128]{1,0:T(8,128)(2,1)S(1)}, u32[]{:S(2)}, u32[]{:S(2)}) %collective-permute-start.23) | collective-permute-done | bytes 233504 | tf_op jit(solution)/shard_map/ppermute | solution.py:30
  105.3 2.9 %collective-permute-start.28 = (bf16[64,1280]{1,0:T(8,128)(2,1)S(1)}, bf16[64,1280]{1,0:T(8,128)(2,1)S(1)}, u32[]{:S(2)}, u32[]{:S(2)}) collective-permute-start(bf16[64,1280]{1,0:T(8,128)(2,1)S(1)} %get-tuple-element.81), channel_id=1, source_target_pairs={{0,16},{8,24},{16,0},{24,8},{1,17},{9,25},{17,1},{25,9},{2,18},{10... | collective-permute-start | bytes 491528 | tf_op jit(solution)/shard_map/ppermute | solution.py:30
  108.9 3.2 %collective-permute-start.33 = (bf16[448,128]{1,0:T(8,128)(2,1)S(1)}, bf16[448,128]{1,0:T(8,128)(2,1)S(1)}, u32[]{:S(2)}, u32[]{:S(2)}) collective-permute-start(bf16[448,128]{1,0:T(8,128)(2,1)S(1)} %get-tuple-element.94.a_0_), channel_id=1, source_target_pairs={{0,128},{64,192},{128,0},{192,64},{1,129},{65,193},{129,1},{193,65... | collective-permute-start | bytes 344072 | tf_op jit(solution)/shard_map/ppermute | solution.py:30
  113.8 2.1 %shard_map.113 = bf16[1024,896]{1,0:T(8,128)(2,1)} custom-call(bf16[912,128]{1,0:T(8,128)(2,1)S(1)} %get-tuple-element.67.a_0_, bf16[912,128]{1,0:T(8,128)(2,1)S(1)} %collective-permute-done.21.a_1_, bf16[912,128]{1,0:T(8,128)(2,1)S(1)} %collective-permute-done.22.a_2_, bf16[912,128]{1,0:T(8,128)(2,1)S(1)} %collective-permute-done.23.a_3_, ...), custom_call_target="tpu_custom_call" | custom-call | tf_op jit(solution)/shard_map/pallas_call | solution.py:80
  115.9 2.1 %shard_map.114 = bf16[1024,896]{1,0:T(8,128)(2,1)} custom-call(bf16[912,128]{1,0:T(8,128)(2,1)S(1)} %get-tuple-element.67.a_0_, bf16[912,128]{1,0:T(8,128)(2,1)S(1)} %collective-permute-done.21.a_1_, bf16[912,128]{1,0:T(8,128)(2,1)S(1)} %collective-permute-done.22.a_2_, bf16[912,128]{1,0:T(8,128)(2,1)S(1)} %collective-permute-done.23.a_3_, ...), custom_call_target="tpu_custom_call" | custom-call | tf_op jit(solution)/shard_map/pallas_call | solution.py:80
  118.3 4.3 %collective-permute-start.30 = (bf16[16,1408]{1,0:T(8,128)(2,1)S(1)}, bf16[16,1408]{1,0:T(8,128)(2,1)S(1)}, u32[]{:S(2)}, u32[]{:S(2)}) collective-permute-start(bf16[16,1408]{1,0:T(8,128)(2,1)S(1)} %get-tuple-element.87), channel_id=1, source_target_pairs={{0,4},{2,6},{4,0},{6,2},{1,5},{3,7},{5,1},{7,3},{8,12},{10,14},{12... | collective-permute-start | bytes 135176 | tf_op jit(solution)/shard_map/ppermute | solution.py:30
  122.6 1.9 %shard_map.116 = bf16[896,1024]{1,0:T(8,128)(2,1)} custom-call(bf16[448,128]{1,0:T(8,128)(2,1)S(1)} %get-tuple-element.94.a_0_, bf16[448,128]{1,0:T(8,128)(2,1)S(1)} %collective-permute-done.32.a_1_, bf16[448,128]{1,0:T(8,128)(2,1)S(1)} %collective-permute-done.33.a_2_, bf16[448,128]{1,0:T(8,128)(2,1)S(1)} %collective-permute-done.34.a_3_, ...), custom_call_target="tpu_custom_call" | custom-call | tf_op jit(solution)/shard_map/pallas_call | solution.py:80
  (69 shorter events, 39.7 us)
Async XLA Ops:
  11.6 9.0 %collective-permute-start.4 = (bf16[4,2,16,1024]{3,2,1,0:T(8,128)(2,1)S(1)}, bf16[4,2,16,1024]{3,2,1,0:T(8,128)(2,1)S(1)}, u32[]{:S(2)}, u32[]{:S(2)}) collective-permute-start(bf16[4,2,16,1024]{3,2,1,0:T(8,128)(2,1)S(1)} %pad_maximum_fusion.a_0_.a_4_), channel_id=1, source_target_pairs={{0,8},{8,16},{16,24},{24,0},{1,9},{9,17},{17,25},{25,1},{2,10},{10... | collective-permute-start | bytes 786440 | tf_op jit(solution)/shard_map/ppermute | solution.py:30
  20.6 9.1 %collective-permute-start.13 = (bf16[4,2,16,1024]{3,2,1,0:T(8,128)(2,1)S(1)}, bf16[4,2,16,1024]{3,2,1,0:T(8,128)(2,1)S(1)}, u32[]{:S(2)}, u32[]{:S(2)}) collective-permute-start(bf16[4,2,16,1024]{3,2,1,0:T(8,128)(2,1)S(1)} %pad_maximum_fusion.a_0_.a_4_), channel_id=1, source_target_pairs={{0,24},{8,0},{16,8},{24,16},{1,25},{9,1},{17,9},{25,17},{2,26},{10... | collective-permute-start | bytes 786440 | tf_op jit(solution)/shard_map/ppermute | solution.py:30
  22.3 9.9 %collective-permute-start.15 = (bf16[4,2,16,1024]{3,2,1,0:T(8,128)(2,1)S(1)}, bf16[4,2,16,1024]{3,2,1,0:T(8,128)(2,1)S(1)}, u32[]{:S(2)}, u32[]{:S(2)}) collective-permute-start(bf16[4,2,16,1024]{3,2,1,0:T(8,128)(2,1)S(1)} %pad_maximum_fusion.a_0_.a_4_), channel_id=1, source_target_pairs={{0,16},{8,24},{16,0},{24,8},{1,17},{9,25},{17,1},{25,9},{2,18},{10... | collective-permute-start | bytes 786440 | tf_op jit(solution)/shard_map/ppermute | solution.py:30
  24.8 13.1 %collective-permute-start.6 = (bf16[1360,128]{1,0:T(8,128)(2,1)S(1)}, bf16[1360,128]{1,0:T(8,128)(2,1)S(1)}, u32[]{:S(2)}, u32[]{:S(2)}) collective-permute-start(bf16[1360,128]{1,0:T(8,128)(2,1)S(1)} %get-tuple-element.55), channel_id=1, source_target_pairs={{0,64},{64,128},{128,192},{192,0},{1,65},{65,129},{129,193},{193,1... | collective-permute-start | bytes 1044488 | tf_op jit(solution)/shard_map/ppermute | solution.py:30
  26.1 17.3 %collective-permute-start.7 = (bf16[1360,128]{1,0:T(8,128)(2,1)S(1)}, bf16[1360,128]{1,0:T(8,128)(2,1)S(1)}, u32[]{:S(2)}, u32[]{:S(2)}) collective-permute-start(bf16[1360,128]{1,0:T(8,128)(2,1)S(1)} %get-tuple-element.56), channel_id=1, source_target_pairs={{0,128},{64,192},{128,0},{192,64},{1,129},{65,193},{129,1},{193,65... | collective-permute-start | bytes 1044488 | tf_op jit(solution)/shard_map/ppermute | solution.py:30
  26.9 18.6 %collective-permute-start.8 = (bf16[1360,128]{1,0:T(8,128)(2,1)S(1)}, bf16[1360,128]{1,0:T(8,128)(2,1)S(1)}, u32[]{:S(2)}, u32[]{:S(2)}) collective-permute-start(bf16[1360,128]{1,0:T(8,128)(2,1)S(1)} %get-tuple-element.57), channel_id=1, source_target_pairs={{0,192},{64,0},{128,64},{192,128},{1,193},{65,1},{129,65},{193,129... | collective-permute-start | bytes 1044488 | tf_op jit(solution)/shard_map/ppermute | solution.py:30
  35.7 16.1 %collective-permute-start.17 = (bf16[1360,128]{1,0:T(8,128)(2,1)S(1)}, bf16[1360,128]{1,0:T(8,128)(2,1)S(1)}, u32[]{:S(2)}, u32[]{:S(2)}) collective-permute-start(bf16[1360,128]{1,0:T(8,128)(2,1)S(1)} %get-tuple-element.62), channel_id=1, source_target_pairs={{0,64},{64,128},{128,192},{192,0},{1,65},{65,129},{129,193},{193,1... | collective-permute-start | bytes 1044488 | tf_op jit(solution)/shard_map/ppermute | solution.py:30
  37.1 20.2 %collective-permute-start.18 = (bf16[1360,128]{1,0:T(8,128)(2,1)S(1)}, bf16[1360,128]{1,0:T(8,128)(2,1)S(1)}, u32[]{:S(2)}, u32[]{:S(2)}) collective-permute-start(bf16[1360,128]{1,0:T(8,128)(2,1)S(1)} %get-tuple-element.63), channel_id=1, source_target_pairs={{0,128},{64,192},{128,0},{192,64},{1,129},{65,193},{129,1},{193,65... | collective-permute-start | bytes 1044488 | tf_op jit(solution)/shard_map/ppermute | solution.py:30
  37.9 21.2 %collective-permute-start.19 = (bf16[1360,128]{1,0:T(8,128)(2,1)S(1)}, bf16[1360,128]{1,0:T(8,128)(2,1)S(1)}, u32[]{:S(2)}, u32[]{:S(2)}) collective-permute-start(bf16[1360,128]{1,0:T(8,128)(2,1)S(1)} %get-tuple-element.64), channel_id=1, source_target_pairs={{0,192},{64,0},{128,64},{192,128},{1,193},{65,1},{129,65},{193,129... | collective-permute-start | bytes 1044488 | tf_op jit(solution)/shard_map/ppermute | solution.py:30
  45.8 19.6 %collective-permute-start.9 = (bf16[1360,128]{1,0:T(8,128)(2,1)S(1)}, bf16[1360,128]{1,0:T(8,128)(2,1)S(1)}, u32[]{:S(2)}, u32[]{:S(2)}) collective-permute-start(bf16[1360,128]{1,0:T(8,128)(2,1)S(1)} %get-tuple-element.59), channel_id=1, source_target_pairs={{0,32},{32,0},{1,33},{33,1},{2,34},{34,2},{3,35},{35,3},{4,36},{36... | collective-permute-start | bytes 1044488 | tf_op jit(solution)/shard_map/ppermute | solution.py:30
  59.5 23.9 %collective-permute-start.20 = (bf16[1360,128]{1,0:T(8,128)(2,1)S(1)}, bf16[1360,128]{1,0:T(8,128)(2,1)S(1)}, u32[]{:S(2)}, u32[]{:S(2)}) collective-permute-start(bf16[1360,128]{1,0:T(8,128)(2,1)S(1)} %get-tuple-element.66), channel_id=1, source_target_pairs={{0,32},{32,0},{1,33},{33,1},{2,34},{34,2},{3,35},{35,3},{4,36},{36... | collective-permute-start | bytes 1044488 | tf_op jit(solution)/shard_map/ppermute | solution.py:30
  65.9 23.3 %collective-permute-start.10 = (bf16[1360,128]{1,0:T(8,128)(2,1)S(1)}, bf16[1360,128]{1,0:T(8,128)(2,1)S(1)}, u32[]{:S(2)}, u32[]{:S(2)}) collective-permute-start(bf16[1360,128]{1,0:T(8,128)(2,1)S(1)} %shard_map.104.a_0_), channel_id=1, source_target_pairs={{0,192},{64,0},{128,64},{192,128},{1,193},{65,1},{129,65},{193,129... | collective-permute-start | bytes 1044488 | tf_op jit(solution)/shard_map/ppermute | solution.py:30
  75.0 14.2 %collective-permute-start.11 = (bf16[1360,128]{1,0:T(8,128)(2,1)S(1)}, bf16[1360,128]{1,0:T(8,128)(2,1)S(1)}, u32[]{:S(2)}, u32[]{:S(2)}) collective-permute-start(bf16[1360,128]{1,0:T(8,128)(2,1)S(1)} %shard_map.104.a_0_), channel_id=1, source_target_pairs={{0,128},{64,192},{128,0},{192,64},{1,129},{65,193},{129,1},{193,65... | collective-permute-start | bytes 1044488 | tf_op jit(solution)/shard_map/ppermute | solution.py:30
  75.0 14.2 %collective-permute-start.12 = (bf16[1360,128]{1,0:T(8,128)(2,1)S(1)}, bf16[1360,128]{1,0:T(8,128)(2,1)S(1)}, u32[]{:S(2)}, u32[]{:S(2)}) collective-permute-start(bf16[1360,128]{1,0:T(8,128)(2,1)S(1)} %shard_map.104.a_0_), channel_id=1, source_target_pairs={{0,64},{64,128},{128,192},{192,0},{1,65},{65,129},{129,193},{193,1... | collective-permute-start | bytes 1044488 | tf_op jit(solution)/shard_map/ppermute | solution.py:30
  83.9 9.8 %collective-permute-start.21 = (bf16[912,128]{1,0:T(8,128)(2,1)S(1)}, bf16[912,128]{1,0:T(8,128)(2,1)S(1)}, u32[]{:S(2)}, u32[]{:S(2)}) collective-permute-start(bf16[912,128]{1,0:T(8,128)(2,1)S(1)} %get-tuple-element.67.a_0_), channel_id=1, source_target_pairs={{0,192},{64,0},{128,64},{192,128},{1,193},{65,1},{129,65},{193,129... | collective-permute-start | bytes 700424 | tf_op jit(solution)/shard_map/ppermute | solution.py:30
  85.1 10.7 %collective-permute-start.22 = (bf16[912,128]{1,0:T(8,128)(2,1)S(1)}, bf16[912,128]{1,0:T(8,128)(2,1)S(1)}, u32[]{:S(2)}, u32[]{:S(2)}) collective-permute-start(bf16[912,128]{1,0:T(8,128)(2,1)S(1)} %get-tuple-element.67.a_0_), channel_id=1, source_target_pairs={{0,128},{64,192},{128,0},{192,64},{1,129},{65,193},{129,1},{193,65... | collective-permute-start | bytes 700424 | tf_op jit(solution)/shard_map/ppermute | solution.py:30
  89.2 10.2 %collective-permute-start.23 = (bf16[912,128]{1,0:T(8,128)(2,1)S(1)}, bf16[912,128]{1,0:T(8,128)(2,1)S(1)}, u32[]{:S(2)}, u32[]{:S(2)}) collective-permute-start(bf16[912,128]{1,0:T(8,128)(2,1)S(1)} %get-tuple-element.67.a_0_), channel_id=1, source_target_pairs={{0,64},{64,128},{128,192},{192,0},{1,65},{65,129},{129,193},{193,1... | collective-permute-start | bytes 700424 | tf_op jit(solution)/shard_map/ppermute | solution.py:30
  92.6 8.6 %collective-permute-start.24 = (bf16[144,1152]{1,0:T(8,128)(2,1)S(1)}, bf16[144,1152]{1,0:T(8,128)(2,1)S(1)}, u32[]{:S(2)}, u32[]{:S(2)}) collective-permute-start(bf16[144,1152]{1,0:T(8,128)(2,1)S(1)} %get-tuple-element.75), channel_id=1, source_target_pairs={{0,1},{1,0},{2,3},{3,2},{4,5},{5,4},{6,7},{7,6},{8,9},{9,8},{10,11... | collective-permute-start | bytes 995336 | tf_op jit(solution)/shard_map/ppermute | solution.py:30
  103.2 8.9 %collective-permute-start.26 = (bf16[64,1280]{1,0:T(8,128)(2,1)S(1)}, bf16[64,1280]{1,0:T(8,128)(2,1)S(1)}, u32[]{:S(2)}, u32[]{:S(2)}) collective-permute-start(bf16[64,1280]{1,0:T(8,128)(2,1)S(1)} %get-tuple-element.79), channel_id=1, source_target_pairs={{0,24},{8,0},{16,8},{24,16},{1,25},{9,1},{17,9},{25,17},{2,26},{10... | collective-permute-start | bytes 491528 | tf_op jit(solution)/shard_map/ppermute | solution.py:30
  104.3 13.7 %collective-permute-start.27 = (bf16[64,1280]{1,0:T(8,128)(2,1)S(1)}, bf16[64,1280]{1,0:T(8,128)(2,1)S(1)}, u32[]{:S(2)}, u32[]{:S(2)}) collective-permute-start(bf16[64,1280]{1,0:T(8,128)(2,1)S(1)} %get-tuple-element.80), channel_id=1, source_target_pairs={{0,8},{8,16},{16,24},{24,0},{1,9},{9,17},{17,25},{25,1},{2,10},{10... | collective-permute-start | bytes 491528 | tf_op jit(solution)/shard_map/ppermute | solution.py:30
  105.3 12.7 %collective-permute-start.28 = (bf16[64,1280]{1,0:T(8,128)(2,1)S(1)}, bf16[64,1280]{1,0:T(8,128)(2,1)S(1)}, u32[]{:S(2)}, u32[]{:S(2)}) collective-permute-start(bf16[64,1280]{1,0:T(8,128)(2,1)S(1)} %get-tuple-element.81), channel_id=1, source_target_pairs={{0,16},{8,24},{16,0},{24,8},{1,17},{9,25},{17,1},{25,9},{2,18},{10... | collective-permute-start | bytes 491528 | tf_op jit(solution)/shard_map/ppermute | solution.py:30
  108.2 14.3 %collective-permute-start.32 = (bf16[448,128]{1,0:T(8,128)(2,1)S(1)}, bf16[448,128]{1,0:T(8,128)(2,1)S(1)}, u32[]{:S(2)}, u32[]{:S(2)}) collective-permute-start(bf16[448,128]{1,0:T(8,128)(2,1)S(1)} %get-tuple-element.94.a_0_), channel_id=1, source_target_pairs={{0,192},{64,0},{128,64},{192,128},{1,193},{65,1},{129,65},{193,129... | collective-permute-start | bytes 344072 | tf_op jit(solution)/shard_map/ppermute | solution.py:30
  108.9 13.7 %collective-permute-start.33 = (bf16[448,128]{1,0:T(8,128)(2,1)S(1)}, bf16[448,128]{1,0:T(8,128)(2,1)S(1)}, u32[]{:S(2)}, u32[]{:S(2)}) collective-permute-start(bf16[448,128]{1,0:T(8,128)(2,1)S(1)} %get-tuple-element.94.a_0_), channel_id=1, source_target_pairs={{0,128},{64,192},{128,0},{192,64},{1,129},{65,193},{129,1},{193,65... | collective-permute-start | bytes 344072 | tf_op jit(solution)/shard_map/ppermute | solution.py:30
  112.1 10.5 %collective-permute-start.34 = (bf16[448,128]{1,0:T(8,128)(2,1)S(1)}, bf16[448,128]{1,0:T(8,128)(2,1)S(1)}, u32[]{:S(2)}, u32[]{:S(2)}) collective-permute-start(bf16[448,128]{1,0:T(8,128)(2,1)S(1)} %get-tuple-element.94.a_0_), channel_id=1, source_target_pairs={{0,64},{64,128},{128,192},{192,0},{1,65},{65,129},{129,193},{193,1... | collective-permute-start | bytes 344072 | tf_op jit(solution)/shard_map/ppermute | solution.py:30
  (13 other events, 68.3 us)

commit v4 on v3

--- a/solution.py
+++ b/solution.py
@@ -355,7 +355,7 @@
         total, out = call(
             add_x,
             [((3 * size + END, LANES), F32), ((3 * size + END, LANES), BF)],
-            [s0, send(s1, "x", 1), send(s2, "x", 2), send(s3, "x", -1)],
+            [s0, send(s2, "x", 2), send(s1, "x", 1), send(s3, "x", -1)],
         )
         totals.append(total)
         crossed.append(send(out, "zh", 1))
@@ -371,7 +371,8 @@
         else:
             shapes = [((2 * cut + END, LANES), BF), ((cut, LANES), BF)]
         m0, *hidden = call(activate, shapes, [total, arrived])
-        found = [m0, send(m0, "x", -1), send(m0, "x", 2), send(m0, "x", 1)]
+        across = send(m0, "x", 2)
+        found = [m0, send(m0, "x", -1), across, send(m0, "x", 1)]
         mine, theirs, inv, gains = call(
             lambda *a, n=size: backward(n, *a),
             [((64 * size, deep), F32), ((64 * size + END, deep), BF), ((4, tall, 1), F32)]
@@ -396,7 +397,8 @@
         [((64, deep + LANES), BF)] * 4,
         [*[h[0] for h in halves], *[h[1] for h in halves], gains],
     )
-    parts = [parts[0]] + [send(parts[i], "y", -STEPS[i]) for i in (1, 2, 3)]
+    sent = {i: send(parts[i], "y", -STEPS[i]) for i in (3, 1, 2)}
+    parts = [parts[0], sent[1], sent[2], sent[3]]
     gain_sum, *outs = call(
         add_y,
         [((1, depth), F32), ((16, deep), F32)] + [((16, deep + 2 * LANES), BF)] * 3,

time: 128 us -> 127 us (level)
  starting transfers between devices: 60.8 us -> 52.6 us
  waiting for transfers between devices: 44.8 us -> 52.6 us
    ppermute x35, starting transfers between devices: 60.8 us -> 52.6 us  [send(): lax.ppermute(value, axis, ring(2 if axis in ('zh', 'core') else 4, step))]
    ppermute x35, waiting for transfers between devices: 44.8 us -> 52.6 us  [send(): lax.ppermute(value, axis, ring(2 if axis in ('zh', 'core') else 4, step))]
where the time goes in v4:
time: 127 us
  starting transfers between devices  52.6 us (41%)
  waiting for transfers between devices  52.6 us (41%)
  Pallas kernels  20.1 us (16%)
    ppermute x35, waiting for transfers between devices, send(): lax.ppermute(value, axis, ring(2 if axis in ('zh', 'core') else 4, step))  52.6 us
    ppermute x35, starting transfers between devices, send(): lax.ppermute(value, axis, ring(2 if axis in ('zh', 'core') else 4, step))  52.6 us
    pallas_call x15, Pallas kernels, call(): pl.pallas_call(kernel, out_shape=[jax.ShapeDtypeStruct(s, d) for s, d in...  17.5 us
    pallas_call x1, Pallas kernels, load(): pl.pallas_call(kernel, out_shape=[jax.ShapeDtypeStruct(w.shape, w.dtype)...  2.64 us
  transfers between devices with their start and end apart: 35, of which 18 were waited for; matrix products, arithmetic and copies ran while one was open for 0% of the time, Pallas kernels for 15%

profile of v4, /device:TPU:4, one launch (start us, length us, event | category | flops | bytes accessed | tf_op | source)
XLA Modules:
  0.0 127.0 jit_solution(7206692880142894014)
XLA Ops:
  3.4 3.3 %collective-permute-start.1 = (bf16[2,16,1024]{2,1,0:T(8,128)(2,1)S(1)}, bf16[2,16,1024]{2,1,0:T(8,128)(2,1)S(1)}, u32[]{:S(2)}, u32[]{:S(2)}) collective-permute-start(bf16[2,16,1024]{2,1,0:T(8,128)(2,1)S(1)} %get-tuple-element.96), channel_id=1, source_target_pairs={{0,4},{2,6},{4,0},{6,2},{1,5},{3,7},{5,1},{7,3},{8,12},{10,14},{12... | collective-permute-start | bytes 196616 | tf_op jit(solution)/shard_map/ppermute | solution.py:30
  8.9 2.3 %collective-permute-done.1 = bf16[2,16,1024]{2,1,0:T(8,128)(2,1)S(1)} collective-permute-done((bf16[2,16,1024]{2,1,0:T(8,128)(2,1)S(1)}, bf16[2,16,1024]{2,1,0:T(8,128)(2,1)S(1)}, u32[]{:S(2)}, u32[]{:S(2)}) %collective-permute-start.1) | collective-permute-done | bytes 65568 | tf_op jit(solution)/shard_map/ppermute | solution.py:30
  13.2 2.6 %shard_map.101 = (bf16[1024,896]{1,0:T(8,128)(2,1)S(1)}, bf16[1024,896]{1,0:T(8,128)(2,1)S(1)}, bf16[896,1024]{1,0:T(8,128)(2,1)S(1)}) custom-call(bf16[1024,896]{1,0:T(8,128)(2,1)} %refs_0_.1, bf16[1024,896]{1,0:T(8,128)(2,1)} %refs_1_.1, bf16[896,1024]{1,0:T(8,128)(2,1)} %refs_2_.1), custom_call_target="tpu_custom_call" | custom-call | tf_op jit(solution)/shard_map/pallas_call | solution.py:104
  16.0 4.6 %collective-permute-done.4.a_2_.a_6_ = bf16[4,2,16,1024]{3,2,1,0:T(8,128)(2,1)S(1)} collective-permute-done((bf16[4,2,16,1024]{3,2,1,0:T(8,128)(2,1)S(1)}, bf16[4,2,16,1024]{3,2,1,0:T(8,128)(2,1)S(1)}, u32[]{:S(2)}, u32[]{:S(2)}) %collective-permute-start.4) | collective-permute-done | bytes 262176 | tf_op jit(solution)/shard_map/ppermute | solution.py:30
  25.4 2.1 %collective-permute-start.7 = (bf16[1360,128]{1,0:T(8,128)(2,1)S(1)}, bf16[1360,128]{1,0:T(8,128)(2,1)S(1)}, u32[]{:S(2)}, u32[]{:S(2)}) collective-permute-start(bf16[1360,128]{1,0:T(8,128)(2,1)S(1)} %get-tuple-element.56), channel_id=1, source_target_pairs={{0,64},{64,128},{128,192},{192,0},{1,65},{65,129},{129,193},{193,1... | collective-permute-start | bytes 1044488 | tf_op jit(solution)/shard_map/ppermute | solution.py:30
  27.6 2.1 %collective-permute-done.13.a_0_.a_4_ = bf16[4,2,16,1024]{3,2,1,0:T(8,128)(2,1)S(1)} collective-permute-done((bf16[4,2,16,1024]{3,2,1,0:T(8,128)(2,1)S(1)}, bf16[4,2,16,1024]{3,2,1,0:T(8,128)(2,1)S(1)}, u32[]{:S(2)}, u32[]{:S(2)}) %collective-permute-start.13) | collective-permute-done | bytes 262176 | tf_op jit(solution)/shard_map/ppermute | solution.py:30
  29.7 2.6 %collective-permute-done.15.a_2_.a_6_ = bf16[4,2,16,1024]{3,2,1,0:T(8,128)(2,1)S(1)} collective-permute-done((bf16[4,2,16,1024]{3,2,1,0:T(8,128)(2,1)S(1)}, bf16[4,2,16,1024]{3,2,1,0:T(8,128)(2,1)S(1)}, u32[]{:S(2)}, u32[]{:S(2)}) %collective-permute-start.15) | collective-permute-done | bytes 262176 | tf_op jit(solution)/shard_map/ppermute | solution.py:30
  36.4 2.1 %collective-permute-start.18 = (bf16[1360,128]{1,0:T(8,128)(2,1)S(1)}, bf16[1360,128]{1,0:T(8,128)(2,1)S(1)}, u32[]{:S(2)}, u32[]{:S(2)}) collective-permute-start(bf16[1360,128]{1,0:T(8,128)(2,1)S(1)} %get-tuple-element.63), channel_id=1, source_target_pairs={{0,64},{64,128},{128,192},{192,0},{1,65},{65,129},{129,193},{193,1... | collective-permute-start | bytes 1044488 | tf_op jit(solution)/shard_map/ppermute | solution.py:30
  38.6 6.4 %collective-permute-done.7.b = bf16[1360,128]{1,0:T(8,128)(2,1)S(1)} collective-permute-done((bf16[1360,128]{1,0:T(8,128)(2,1)S(1)}, bf16[1360,128]{1,0:T(8,128)(2,1)S(1)}, u32[]{:S(2)}, u32[]{:S(2)}) %collective-permute-start.7) | collective-permute-done | bytes 348192 | tf_op jit(solution)/shard_map/ppermute | solution.py:30
  45.3 5.9 %collective-permute-start.9 = (bf16[1360,128]{1,0:T(8,128)(2,1)S(1)}, bf16[1360,128]{1,0:T(8,128)(2,1)S(1)}, u32[]{:S(2)}, u32[]{:S(2)}) collective-permute-start(bf16[1360,128]{1,0:T(8,128)(2,1)S(1)} %get-tuple-element.59), channel_id=1, source_target_pairs={{0,32},{32,0},{1,33},{33,1},{2,34},{34,2},{3,35},{35,3},{4,36},{36... | collective-permute-start | bytes 1044488 | tf_op jit(solution)/shard_map/ppermute | solution.py:30
  52.4 5.5 %collective-permute-done.18.b = bf16[1360,128]{1,0:T(8,128)(2,1)S(1)} collective-permute-done((bf16[1360,128]{1,0:T(8,128)(2,1)S(1)}, bf16[1360,128]{1,0:T(8,128)(2,1)S(1)}, u32[]{:S(2)}, u32[]{:S(2)}) %collective-permute-start.18) | collective-permute-done | bytes 348192 | tf_op jit(solution)/shard_map/ppermute | solution.py:30
  58.3 5.9 %collective-permute-start.20 = (bf16[1360,128]{1,0:T(8,128)(2,1)S(1)}, bf16[1360,128]{1,0:T(8,128)(2,1)S(1)}, u32[]{:S(2)}, u32[]{:S(2)}) collective-permute-start(bf16[1360,128]{1,0:T(8,128)(2,1)S(1)} %get-tuple-element.66), channel_id=1, source_target_pairs={{0,32},{32,0},{1,33},{33,1},{2,34},{34,2},{3,35},{35,3},{4,36},{36... | collective-permute-start | bytes 1044488 | tf_op jit(solution)/shard_map/ppermute | solution.py:30
  66.3 2.6 %collective-permute-start.11 = (bf16[1360,128]{1,0:T(8,128)(2,1)S(1)}, bf16[1360,128]{1,0:T(8,128)(2,1)S(1)}, u32[]{:S(2)}, u32[]{:S(2)}) collective-permute-start(bf16[1360,128]{1,0:T(8,128)(2,1)S(1)} %shard_map.104.a_0_), channel_id=1, source_target_pairs={{0,128},{64,192},{128,0},{192,64},{1,129},{65,193},{129,1},{193,65... | collective-permute-start | bytes 1044488 | tf_op jit(solution)/shard_map/ppermute | solution.py:30
  68.9 13.9 %collective-permute-done.20.other = bf16[1360,128]{1,0:T(8,128)(2,1)S(1)} collective-permute-done((bf16[1360,128]{1,0:T(8,128)(2,1)S(1)}, bf16[1360,128]{1,0:T(8,128)(2,1)S(1)}, u32[]{:S(2)}, u32[]{:S(2)}) %collective-permute-start.20) | collective-permute-done | bytes 348192 | tf_op jit(solution)/shard_map/ppermute | solution.py:30
  83.3 3.0 %collective-permute-start.21 = (bf16[912,128]{1,0:T(8,128)(2,1)S(1)}, bf16[912,128]{1,0:T(8,128)(2,1)S(1)}, u32[]{:S(2)}, u32[]{:S(2)}) collective-permute-start(bf16[912,128]{1,0:T(8,128)(2,1)S(1)} %get-tuple-element.67.a_0_), channel_id=1, source_target_pairs={{0,192},{64,0},{128,64},{192,128},{1,193},{65,1},{129,65},{193,129... | collective-permute-start | bytes 700424 | tf_op jit(solution)/shard_map/ppermute | solution.py:30
  86.3 2.7 %collective-permute-start.22 = (bf16[912,128]{1,0:T(8,128)(2,1)S(1)}, bf16[912,128]{1,0:T(8,128)(2,1)S(1)}, u32[]{:S(2)}, u32[]{:S(2)}) collective-permute-start(bf16[912,128]{1,0:T(8,128)(2,1)S(1)} %get-tuple-element.67.a_0_), channel_id=1, source_target_pairs={{0,128},{64,192},{128,0},{192,64},{1,129},{65,193},{129,1},{193,65... | collective-permute-start | bytes 700424 | tf_op jit(solution)/shard_map/ppermute | solution.py:30
  93.4 3.0 %collective-permute-done.22.a_2_ = bf16[912,128]{1,0:T(8,128)(2,1)S(1)} collective-permute-done((bf16[912,128]{1,0:T(8,128)(2,1)S(1)}, bf16[912,128]{1,0:T(8,128)(2,1)S(1)}, u32[]{:S(2)}, u32[]{:S(2)}) %collective-permute-start.22) | collective-permute-done | bytes 233504 | tf_op jit(solution)/shard_map/ppermute | solution.py:30
  96.4 3.6 %collective-permute-done.23.a_3_ = bf16[912,128]{1,0:T(8,128)(2,1)S(1)} collective-permute-done((bf16[912,128]{1,0:T(8,128)(2,1)S(1)}, bf16[912,128]{1,0:T(8,128)(2,1)S(1)}, u32[]{:S(2)}, u32[]{:S(2)}) %collective-permute-start.23) | collective-permute-done | bytes 233504 | tf_op jit(solution)/shard_map/ppermute | solution.py:30
  105.7 2.9 %collective-permute-start.28 = (bf16[64,1280]{1,0:T(8,128)(2,1)S(1)}, bf16[64,1280]{1,0:T(8,128)(2,1)S(1)}, u32[]{:S(2)}, u32[]{:S(2)}) collective-permute-start(bf16[64,1280]{1,0:T(8,128)(2,1)S(1)} %get-tuple-element.81), channel_id=1, source_target_pairs={{0,16},{8,24},{16,0},{24,8},{1,17},{9,25},{17,1},{25,9},{2,18},{10... | collective-permute-start | bytes 491528 | tf_op jit(solution)/shard_map/ppermute | solution.py:30
  109.2 2.7 %collective-permute-start.33 = (bf16[448,128]{1,0:T(8,128)(2,1)S(1)}, bf16[448,128]{1,0:T(8,128)(2,1)S(1)}, u32[]{:S(2)}, u32[]{:S(2)}) collective-permute-start(bf16[448,128]{1,0:T(8,128)(2,1)S(1)} %get-tuple-element.94.a_0_), channel_id=1, source_target_pairs={{0,128},{64,192},{128,0},{192,64},{1,129},{65,193},{129,1},{193,65... | collective-permute-start | bytes 344072 | tf_op jit(solution)/shard_map/ppermute | solution.py:30
  112.0 2.0 %collective-permute-start.34 = (bf16[448,128]{1,0:T(8,128)(2,1)S(1)}, bf16[448,128]{1,0:T(8,128)(2,1)S(1)}, u32[]{:S(2)}, u32[]{:S(2)}) collective-permute-start(bf16[448,128]{1,0:T(8,128)(2,1)S(1)} %get-tuple-element.94.a_0_), channel_id=1, source_target_pairs={{0,64},{64,128},{128,192},{192,0},{1,65},{65,129},{129,193},{193,1... | collective-permute-start | bytes 344072 | tf_op jit(solution)/shard_map/ppermute | solution.py:30
  114.0 2.1 %shard_map.113 = bf16[1024,896]{1,0:T(8,128)(2,1)} custom-call(bf16[912,128]{1,0:T(8,128)(2,1)S(1)} %get-tuple-element.67.a_0_, bf16[912,128]{1,0:T(8,128)(2,1)S(1)} %collective-permute-done.21.a_1_, bf16[912,128]{1,0:T(8,128)(2,1)S(1)} %collective-permute-done.22.a_2_, bf16[912,128]{1,0:T(8,128)(2,1)S(1)} %collective-permute-done.23.a_3_, ...), custom_call_target="tpu_custom_call" | custom-call | tf_op jit(solution)/shard_map/pallas_call | solution.py:80
  116.1 2.1 %shard_map.114 = bf16[1024,896]{1,0:T(8,128)(2,1)} custom-call(bf16[912,128]{1,0:T(8,128)(2,1)S(1)} %get-tuple-element.67.a_0_, bf16[912,128]{1,0:T(8,128)(2,1)S(1)} %collective-permute-done.21.a_1_, bf16[912,128]{1,0:T(8,128)(2,1)S(1)} %collective-permute-done.22.a_2_, bf16[912,128]{1,0:T(8,128)(2,1)S(1)} %collective-permute-done.23.a_3_, ...), custom_call_target="tpu_custom_call" | custom-call | tf_op jit(solution)/shard_map/pallas_call | solution.py:80
  118.4 3.7 %collective-permute-start.30 = (bf16[16,1408]{1,0:T(8,128)(2,1)S(1)}, bf16[16,1408]{1,0:T(8,128)(2,1)S(1)}, u32[]{:S(2)}, u32[]{:S(2)}) collective-permute-start(bf16[16,1408]{1,0:T(8,128)(2,1)S(1)} %get-tuple-element.87), channel_id=1, source_target_pairs={{0,4},{2,6},{4,0},{6,2},{1,5},{3,7},{5,1},{7,3},{8,12},{10,14},{12... | collective-permute-start | bytes 135176 | tf_op jit(solution)/shard_map/ppermute | solution.py:30
  (69 shorter events, 36.4 us)
Async XLA Ops:
  11.6 9.0 %collective-permute-start.4 = (bf16[4,2,16,1024]{3,2,1,0:T(8,128)(2,1)S(1)}, bf16[4,2,16,1024]{3,2,1,0:T(8,128)(2,1)S(1)}, u32[]{:S(2)}, u32[]{:S(2)}) collective-permute-start(bf16[4,2,16,1024]{3,2,1,0:T(8,128)(2,1)S(1)} %pad_maximum_fusion.a_0_.a_4_), channel_id=1, source_target_pairs={{0,8},{8,16},{16,24},{24,0},{1,9},{9,17},{17,25},{25,1},{2,10},{10... | collective-permute-start | bytes 786440 | tf_op jit(solution)/shard_map/ppermute | solution.py:30
  20.6 9.1 %collective-permute-start.13 = (bf16[4,2,16,1024]{3,2,1,0:T(8,128)(2,1)S(1)}, bf16[4,2,16,1024]{3,2,1,0:T(8,128)(2,1)S(1)}, u32[]{:S(2)}, u32[]{:S(2)}) collective-permute-start(bf16[4,2,16,1024]{3,2,1,0:T(8,128)(2,1)S(1)} %pad_maximum_fusion.a_0_.a_4_), channel_id=1, source_target_pairs={{0,24},{8,0},{16,8},{24,16},{1,25},{9,1},{17,9},{25,17},{2,26},{10... | collective-permute-start | bytes 786440 | tf_op jit(solution)/shard_map/ppermute | solution.py:30
  22.3 9.9 %collective-permute-start.15 = (bf16[4,2,16,1024]{3,2,1,0:T(8,128)(2,1)S(1)}, bf16[4,2,16,1024]{3,2,1,0:T(8,128)(2,1)S(1)}, u32[]{:S(2)}, u32[]{:S(2)}) collective-permute-start(bf16[4,2,16,1024]{3,2,1,0:T(8,128)(2,1)S(1)} %pad_maximum_fusion.a_0_.a_4_), channel_id=1, source_target_pairs={{0,16},{8,24},{16,0},{24,8},{1,17},{9,25},{17,1},{25,9},{2,18},{10... | collective-permute-start | bytes 786440 | tf_op jit(solution)/shard_map/ppermute | solution.py:30
  24.8 13.7 %collective-permute-start.6 = (bf16[1360,128]{1,0:T(8,128)(2,1)S(1)}, bf16[1360,128]{1,0:T(8,128)(2,1)S(1)}, u32[]{:S(2)}, u32[]{:S(2)}) collective-permute-start(bf16[1360,128]{1,0:T(8,128)(2,1)S(1)} %get-tuple-element.55), channel_id=1, source_target_pairs={{0,128},{64,192},{128,0},{192,64},{1,129},{65,193},{129,1},{193,65... | collective-permute-start | bytes 1044488 | tf_op jit(solution)/shard_map/ppermute | solution.py:30
  25.4 19.5 %collective-permute-start.7 = (bf16[1360,128]{1,0:T(8,128)(2,1)S(1)}, bf16[1360,128]{1,0:T(8,128)(2,1)S(1)}, u32[]{:S(2)}, u32[]{:S(2)}) collective-permute-start(bf16[1360,128]{1,0:T(8,128)(2,1)S(1)} %get-tuple-element.56), channel_id=1, source_target_pairs={{0,64},{64,128},{128,192},{192,0},{1,65},{65,129},{129,193},{193,1... | collective-permute-start | bytes 1044488 | tf_op jit(solution)/shard_map/ppermute | solution.py:30
  27.5 17.4 %collective-permute-start.8 = (bf16[1360,128]{1,0:T(8,128)(2,1)S(1)}, bf16[1360,128]{1,0:T(8,128)(2,1)S(1)}, u32[]{:S(2)}, u32[]{:S(2)}) collective-permute-start(bf16[1360,128]{1,0:T(8,128)(2,1)S(1)} %get-tuple-element.57), channel_id=1, source_target_pairs={{0,192},{64,0},{128,64},{192,128},{1,193},{65,1},{129,65},{193,129... | collective-permute-start | bytes 1044488 | tf_op jit(solution)/shard_map/ppermute | solution.py:30
  35.7 16.7 %collective-permute-start.17 = (bf16[1360,128]{1,0:T(8,128)(2,1)S(1)}, bf16[1360,128]{1,0:T(8,128)(2,1)S(1)}, u32[]{:S(2)}, u32[]{:S(2)}) collective-permute-start(bf16[1360,128]{1,0:T(8,128)(2,1)S(1)} %get-tuple-element.62), channel_id=1, source_target_pairs={{0,128},{64,192},{128,0},{192,64},{1,129},{65,193},{129,1},{193,65... | collective-permute-start | bytes 1044488 | tf_op jit(solution)/shard_map/ppermute | solution.py:30
  36.4 21.5 %collective-permute-start.18 = (bf16[1360,128]{1,0:T(8,128)(2,1)S(1)}, bf16[1360,128]{1,0:T(8,128)(2,1)S(1)}, u32[]{:S(2)}, u32[]{:S(2)}) collective-permute-start(bf16[1360,128]{1,0:T(8,128)(2,1)S(1)} %get-tuple-element.63), channel_id=1, source_target_pairs={{0,64},{64,128},{128,192},{192,0},{1,65},{65,129},{129,193},{193,1... | collective-permute-start | bytes 1044488 | tf_op jit(solution)/shard_map/ppermute | solution.py:30
  38.5 19.4 %collective-permute-start.19 = (bf16[1360,128]{1,0:T(8,128)(2,1)S(1)}, bf16[1360,128]{1,0:T(8,128)(2,1)S(1)}, u32[]{:S(2)}, u32[]{:S(2)}) collective-permute-start(bf16[1360,128]{1,0:T(8,128)(2,1)S(1)} %get-tuple-element.64), channel_id=1, source_target_pairs={{0,192},{64,0},{128,64},{192,128},{1,193},{65,1},{129,65},{193,129... | collective-permute-start | bytes 1044488 | tf_op jit(solution)/shard_map/ppermute | solution.py:30
  45.3 18.9 %collective-permute-start.9 = (bf16[1360,128]{1,0:T(8,128)(2,1)S(1)}, bf16[1360,128]{1,0:T(8,128)(2,1)S(1)}, u32[]{:S(2)}, u32[]{:S(2)}) collective-permute-start(bf16[1360,128]{1,0:T(8,128)(2,1)S(1)} %get-tuple-element.59), channel_id=1, source_target_pairs={{0,32},{32,0},{1,33},{33,1},{2,34},{34,2},{3,35},{35,3},{4,36},{36... | collective-permute-start | bytes 1044488 | tf_op jit(solution)/shard_map/ppermute | solution.py:30
  58.3 24.5 %collective-permute-start.20 = (bf16[1360,128]{1,0:T(8,128)(2,1)S(1)}, bf16[1360,128]{1,0:T(8,128)(2,1)S(1)}, u32[]{:S(2)}, u32[]{:S(2)}) collective-permute-start(bf16[1360,128]{1,0:T(8,128)(2,1)S(1)} %get-tuple-element.66), channel_id=1, source_target_pairs={{0,32},{32,0},{1,33},{33,1},{2,34},{34,2},{3,35},{35,3},{4,36},{36... | collective-permute-start | bytes 1044488 | tf_op jit(solution)/shard_map/ppermute | solution.py:30
  64.7 24.3 %collective-permute-start.10 = (bf16[1360,128]{1,0:T(8,128)(2,1)S(1)}, bf16[1360,128]{1,0:T(8,128)(2,1)S(1)}, u32[]{:S(2)}, u32[]{:S(2)}) collective-permute-start(bf16[1360,128]{1,0:T(8,128)(2,1)S(1)} %shard_map.104.a_0_), channel_id=1, source_target_pairs={{0,192},{64,0},{128,64},{192,128},{1,193},{65,1},{129,65},{193,129... | collective-permute-start | bytes 1044488 | tf_op jit(solution)/shard_map/ppermute | solution.py:30
  66.3 22.8 %collective-permute-start.11 = (bf16[1360,128]{1,0:T(8,128)(2,1)S(1)}, bf16[1360,128]{1,0:T(8,128)(2,1)S(1)}, u32[]{:S(2)}, u32[]{:S(2)}) collective-permute-start(bf16[1360,128]{1,0:T(8,128)(2,1)S(1)} %shard_map.104.a_0_), channel_id=1, source_target_pairs={{0,128},{64,192},{128,0},{192,64},{1,129},{65,193},{129,1},{193,65... | collective-permute-start | bytes 1044488 | tf_op jit(solution)/shard_map/ppermute | solution.py:30
  68.9 20.2 %collective-permute-start.12 = (bf16[1360,128]{1,0:T(8,128)(2,1)S(1)}, bf16[1360,128]{1,0:T(8,128)(2,1)S(1)}, u32[]{:S(2)}, u32[]{:S(2)}) collective-permute-start(bf16[1360,128]{1,0:T(8,128)(2,1)S(1)} %shard_map.104.a_0_), channel_id=1, source_target_pairs={{0,64},{64,128},{128,192},{192,0},{1,65},{65,129},{129,193},{193,1... | collective-permute-start | bytes 1044488 | tf_op jit(solution)/shard_map/ppermute | solution.py:30
  83.3 10.1 %collective-permute-start.21 = (bf16[912,128]{1,0:T(8,128)(2,1)S(1)}, bf16[912,128]{1,0:T(8,128)(2,1)S(1)}, u32[]{:S(2)}, u32[]{:S(2)}) collective-permute-start(bf16[912,128]{1,0:T(8,128)(2,1)S(1)} %get-tuple-element.67.a_0_), channel_id=1, source_target_pairs={{0,192},{64,0},{128,64},{192,128},{1,193},{65,1},{129,65},{193,129... | collective-permute-start | bytes 700424 | tf_op jit(solution)/shard_map/ppermute | solution.py:30
  86.3 10.2 %collective-permute-start.22 = (bf16[912,128]{1,0:T(8,128)(2,1)S(1)}, bf16[912,128]{1,0:T(8,128)(2,1)S(1)}, u32[]{:S(2)}, u32[]{:S(2)}) collective-permute-start(bf16[912,128]{1,0:T(8,128)(2,1)S(1)} %get-tuple-element.67.a_0_), channel_id=1, source_target_pairs={{0,128},{64,192},{128,0},{192,64},{1,129},{65,193},{129,1},{193,65... | collective-permute-start | bytes 700424 | tf_op jit(solution)/shard_map/ppermute | solution.py:30
  89.0 11.0 %collective-permute-start.23 = (bf16[912,128]{1,0:T(8,128)(2,1)S(1)}, bf16[912,128]{1,0:T(8,128)(2,1)S(1)}, u32[]{:S(2)}, u32[]{:S(2)}) collective-permute-start(bf16[912,128]{1,0:T(8,128)(2,1)S(1)} %get-tuple-element.67.a_0_), channel_id=1, source_target_pairs={{0,64},{64,128},{128,192},{192,0},{1,65},{65,129},{129,193},{193,1... | collective-permute-start | bytes 700424 | tf_op jit(solution)/shard_map/ppermute | solution.py:30
  92.4 9.2 %collective-permute-start.24 = (bf16[144,1152]{1,0:T(8,128)(2,1)S(1)}, bf16[144,1152]{1,0:T(8,128)(2,1)S(1)}, u32[]{:S(2)}, u32[]{:S(2)}) collective-permute-start(bf16[144,1152]{1,0:T(8,128)(2,1)S(1)} %get-tuple-element.75), channel_id=1, source_target_pairs={{0,1},{1,0},{2,3},{3,2},{4,5},{5,4},{6,7},{7,6},{8,9},{9,8},{10,11... | collective-permute-start | bytes 995336 | tf_op jit(solution)/shard_map/ppermute | solution.py:30
  103.6 8.4 %collective-permute-start.26 = (bf16[64,1280]{1,0:T(8,128)(2,1)S(1)}, bf16[64,1280]{1,0:T(8,128)(2,1)S(1)}, u32[]{:S(2)}, u32[]{:S(2)}) collective-permute-start(bf16[64,1280]{1,0:T(8,128)(2,1)S(1)} %get-tuple-element.79), channel_id=1, source_target_pairs={{0,24},{8,0},{16,8},{24,16},{1,25},{9,1},{17,9},{25,17},{2,26},{10... | collective-permute-start | bytes 491528 | tf_op jit(solution)/shard_map/ppermute | solution.py:30
  105.2 12.9 %collective-permute-start.27 = (bf16[64,1280]{1,0:T(8,128)(2,1)S(1)}, bf16[64,1280]{1,0:T(8,128)(2,1)S(1)}, u32[]{:S(2)}, u32[]{:S(2)}) collective-permute-start(bf16[64,1280]{1,0:T(8,128)(2,1)S(1)} %get-tuple-element.80), channel_id=1, source_target_pairs={{0,8},{8,16},{16,24},{24,0},{1,9},{9,17},{17,25},{25,1},{2,10},{10... | collective-permute-start | bytes 491528 | tf_op jit(solution)/shard_map/ppermute | solution.py:30
  105.7 12.4 %collective-permute-start.28 = (bf16[64,1280]{1,0:T(8,128)(2,1)S(1)}, bf16[64,1280]{1,0:T(8,128)(2,1)S(1)}, u32[]{:S(2)}, u32[]{:S(2)}) collective-permute-start(bf16[64,1280]{1,0:T(8,128)(2,1)S(1)} %get-tuple-element.81), channel_id=1, source_target_pairs={{0,16},{8,24},{16,0},{24,8},{1,17},{9,25},{17,1},{25,9},{2,18},{10... | collective-permute-start | bytes 491528 | tf_op jit(solution)/shard_map/ppermute | solution.py:30
  108.6 13.5 %collective-permute-start.32 = (bf16[448,128]{1,0:T(8,128)(2,1)S(1)}, bf16[448,128]{1,0:T(8,128)(2,1)S(1)}, u32[]{:S(2)}, u32[]{:S(2)}) collective-permute-start(bf16[448,128]{1,0:T(8,128)(2,1)S(1)} %get-tuple-element.94.a_0_), channel_id=1, source_target_pairs={{0,192},{64,0},{128,64},{192,128},{1,193},{65,1},{129,65},{193,129... | collective-permute-start | bytes 344072 | tf_op jit(solution)/shard_map/ppermute | solution.py:30
  109.2 13.1 %collective-permute-start.33 = (bf16[448,128]{1,0:T(8,128)(2,1)S(1)}, bf16[448,128]{1,0:T(8,128)(2,1)S(1)}, u32[]{:S(2)}, u32[]{:S(2)}) collective-permute-start(bf16[448,128]{1,0:T(8,128)(2,1)S(1)} %get-tuple-element.94.a_0_), channel_id=1, source_target_pairs={{0,128},{64,192},{128,0},{192,64},{1,129},{65,193},{129,1},{193,65... | collective-permute-start | bytes 344072 | tf_op jit(solution)/shard_map/ppermute | solution.py:30
  112.0 10.4 %collective-permute-start.34 = (bf16[448,128]{1,0:T(8,128)(2,1)S(1)}, bf16[448,128]{1,0:T(8,128)(2,1)S(1)}, u32[]{:S(2)}, u32[]{:S(2)}) collective-permute-start(bf16[448,128]{1,0:T(8,128)(2,1)S(1)} %get-tuple-element.94.a_0_), channel_id=1, source_target_pairs={{0,64},{64,128},{128,192},{192,0},{1,65},{65,129},{129,193},{193,1... | collective-permute-start | bytes 344072 | tf_op jit(solution)/shard_map/ppermute | solution.py:30
  (13 other events, 67.7 us)
